TPU v7x, 256 devices: a whole 4x4x8 slice. The times are simulated.
256 devices in a mesh: seq: 64 (over y, z, core), dp: 4 (over x).
Axes of the slice: x: 4, y: 4, z: 8, core: 2. Of those that a mesh axis runs over, the one named last changes fastest.
Arguments:
- tokens: bfloat16 [4, 8192, 768], P('dp', 'seq'), may hold values from -6 to 6
- cotangent: bfloat16 [4, 8192, 768], P('dp', 'seq'), may hold values from -6 to 6
- qkv_weight: bfloat16 [2304, 768], replicated, may hold values from -0.21875 to 0.21875
- out_weight: bfloat16 [768, 768], replicated, may hold values from -0.21875 to 0.21875
- logit_scale: float32 [12], replicated, may hold values from 4 to 24
- near_offsets: int32 [12], replicated, may hold values from 0 to 7
- far_offsets: int32 [12], replicated, may hold values from 0 to 63
Outputs:
- branch: bfloat16 [4, 8192, 768], P('dp', 'seq')
- grad_tokens: bfloat16 [4, 8192, 768], P('dp', 'seq')
- qkv_grad: float32 [2304, 768], P(('seq', 'dp'))
- out_grad: float32 [768, 768], P(('seq', 'dp'))
All inputs are finite; a program needn't handle non-finite values.
Results may differ from a plain program's by a relative error of at most 0.014.
Values may be sent and summed in bfloat16 or wider, within the bound.
A program may use at most 128 MiB of HBM per device.

v0:
```python
import jax
import jax.numpy as jnp
from jax import lax
from jax.sharding import PartitionSpec as P

NEAR_BITS = 3
SPAN = 8


EPS = 1e-06


def from_partner(block, axis, bit):
    count = lax.axis_size(axis)
    route = []
    for low in range(count):
        high = low | 1 << bit
        if high != low and high < count:
            route += [(low, high), (high, low)]
    return lax.ppermute(block, axis, route)


def level_mask(offsets, dilation):
    return jnp.arange(dilation, dtype=jnp.int32)[:, None] == offsets[None, :]


def dilate(values, pick_mask):
    dilation = pick_mask.shape[0]
    shaped = values.reshape((values.shape[0] // dilation, dilation) + values.shape[1:])
    pick = pick_mask.reshape(pick_mask.shape + (1,) * (values.ndim - 2))
    return jnp.sum(jnp.where(pick[None], shaped, jnp.zeros((), values.dtype)), axis=1)


def undilate(values, pick_mask):
    dilation = pick_mask.shape[0]
    pick = pick_mask.reshape(pick_mask.shape + (1,) * (values.ndim - 2))
    spread = jnp.where(pick[None], values[:, None], jnp.zeros((), values.dtype))
    return spread.reshape((values.shape[0] * dilation,) + values.shape[1:])


def block_forward(query_rows, key_rows, value_rows, logit_scale):
    scores = (
        jnp.einsum("qhe,khe->hqk", query_rows, key_rows, preferred_element_type=jnp.float32)
        * logit_scale[:, None, None]
    )
    weights = jnp.exp(scores)
    denominator = jnp.sum(weights, axis=2).T
    numerator = jnp.einsum(
        "hqk,khe->qhe", weights.astype(jnp.bfloat16), value_rows, preferred_element_type=jnp.float32
    )
    return (numerator, denominator)


def block_backward(
    query_rows, key_rows, value_rows, grad_rows, row_delta, inverse_den, logit_scale
):
    scores = (
        jnp.einsum("qhe,khe->hqk", query_rows, key_rows, preferred_element_type=jnp.float32)
        * logit_scale[:, None, None]
    )
    probs = jnp.exp(scores) * inverse_den.T[:, :, None]
    grad_probs = jnp.einsum(
        "qhe,khe->hqk", grad_rows, value_rows, preferred_element_type=jnp.float32
    )
    grad_scores = (
        logit_scale[:, None, None] * probs * (grad_probs - row_delta.T[:, :, None])
    ).astype(jnp.bfloat16)
    grad_query = jnp.einsum(
        "hqk,khe->qhe", grad_scores, key_rows, preferred_element_type=jnp.float32
    )
    grad_key = jnp.einsum(
        "hqk,qhe->khe", grad_scores, query_rows, preferred_element_type=jnp.float32
    )
    grad_value = jnp.einsum(
        "hqk,qhe->khe", probs.astype(jnp.bfloat16), grad_rows, preferred_element_type=jnp.float32
    )
    return (grad_query, grad_key, grad_value)


def normalize(rows):
    wide = rows.astype(jnp.float32)
    inverse = lax.rsqrt(jnp.sum(wide * wide, axis=-1) + EPS)
    return (inverse, wide * inverse[..., None])


def unnormalize(inverse, unit, grad_unit):
    return inverse[..., None] * (
        grad_unit - unit * jnp.sum(unit * grad_unit, axis=-1, keepdims=True)
    )


def doubling(packet, device_index):
    for bit_number in range(NEAR_BITS):
        partner = from_partner(packet, "seq", bit_number)
        upper_half = device_index >> bit_number & 1 == 1
        packet = jnp.where(
            upper_half,
            jnp.concatenate([partner, packet], axis=0),
            jnp.concatenate([packet, partner], axis=0),
        )
    return packet


def halving(packet, device_index):
    for bit_number in reversed(range(NEAR_BITS)):
        half_rows = packet.shape[0] // 2
        upper_half = device_index >> bit_number & 1 == 1
        kept = jnp.where(upper_half, packet[half_rows:], packet[:half_rows])
        given = jnp.where(upper_half, packet[:half_rows], packet[half_rows:])
        packet = kept + from_partner(given.astype(jnp.bfloat16), "seq", bit_number).astype(
            given.dtype
        )
    return packet


def pack_rows(first_rows, second_rows, width):
    return jnp.stack([first_rows.reshape(-1, width), second_rows.reshape(-1, width)], axis=1)


def body(tokens, cotangent, qkv_weight, out_weight, logit_scale, near_offsets, far_offsets):
    token_rows = tokens.shape[1]
    width = tokens.shape[2]
    head_count = logit_scale.shape[0]
    head_size = width // head_count
    seq_count = lax.axis_size("seq")
    device_index = lax.axis_index("seq")
    inputs = tokens[0]
    incoming = cotangent[0]
    qkv = lax.dot_general(
        inputs, qkv_weight, (((1,), (1,)), ((), ())), preferred_element_type=jnp.float32
    ).astype(jnp.bfloat16)
    query = qkv[:, :width].reshape(token_rows, head_count, head_size)
    key = qkv[:, width : 2 * width].reshape(token_rows, head_count, head_size)
    value = qkv[:, 2 * width :].reshape(token_rows, head_count, head_size)
    query_inverse, query_unit = normalize(query)
    key_inverse, key_unit = normalize(key)
    query_norm = query_unit.astype(jnp.bfloat16)
    key_norm = key_unit.astype(jnp.bfloat16)
    near_mask = level_mask(near_offsets, SPAN)
    far_mask = level_mask(far_offsets, seq_count)
    near_packet = doubling(
        pack_rows(dilate(key_norm, near_mask), dilate(value, near_mask), width), device_index
    )
    far_packet = lax.all_gather(
        pack_rows(dilate(key_norm, far_mask), dilate(value, far_mask), width),
        "seq",
        axis=0,
        tiled=True,
    )
    near_keys = near_packet[:, 0].reshape(-1, head_count, head_size)
    near_values = near_packet[:, 1].reshape(-1, head_count, head_size)
    far_keys = far_packet[:, 0].reshape(-1, head_count, head_size)
    far_values = far_packet[:, 1].reshape(-1, head_count, head_size)
    near_queries = dilate(query_norm, near_mask)
    far_queries = dilate(query_norm, far_mask)
    numerator, denominator = block_forward(query_norm, key_norm, value, logit_scale)
    near_num, near_den = block_forward(near_queries, near_keys, near_values, logit_scale)
    far_num, far_den = block_forward(far_queries, far_keys, far_values, logit_scale)
    numerator = numerator + undilate(near_num, near_mask) + undilate(far_num, far_mask)
    denominator = denominator + undilate(near_den, near_mask) + undilate(far_den, far_mask)
    attn = (numerator / denominator[..., None]).astype(jnp.bfloat16)
    attn_flat = attn.reshape(token_rows, width)
    branch = jnp.dot(attn_flat, out_weight, preferred_element_type=jnp.float32).astype(jnp.bfloat16)
    grad_attn = lax.dot_general(
        incoming, out_weight, (((1,), (1,)), ((), ())), preferred_element_type=jnp.float32
    ).astype(jnp.bfloat16)
    grad_attn = grad_attn.reshape(token_rows, head_count, head_size)
    row_delta = jnp.sum(grad_attn.astype(jnp.float32) * attn.astype(jnp.float32), axis=-1)
    inverse_den = 1.0 / denominator
    grad_qn, grad_kn, grad_value = block_backward(
        query_norm, key_norm, value, grad_attn, row_delta, inverse_den, logit_scale
    )
    near_gq, near_gk, near_gv = block_backward(
        near_queries,
        near_keys,
        near_values,
        dilate(grad_attn, near_mask),
        dilate(row_delta, near_mask),
        dilate(inverse_den, near_mask),
        logit_scale,
    )
    far_gq, far_gk, far_gv = block_backward(
        far_queries,
        far_keys,
        far_values,
        dilate(grad_attn, far_mask),
        dilate(row_delta, far_mask),
        dilate(inverse_den, far_mask),
        logit_scale,
    )
    near_owned = halving(pack_rows(near_gk, near_gv, width), device_index)
    far_owned = lax.psum_scatter(
        pack_rows(far_gk, far_gv, width), "seq", scatter_dimension=0, tiled=True
    )
    grad_qn = grad_qn + undilate(near_gq, near_mask) + undilate(far_gq, far_mask)
    grad_kn = (
        grad_kn
        + undilate(near_owned[:, 0].reshape(-1, head_count, head_size), near_mask)
        + undilate(far_owned[:, 0].reshape(-1, head_count, head_size), far_mask)
    )
    grad_value = (
        grad_value
        + undilate(near_owned[:, 1].reshape(-1, head_count, head_size), near_mask)
        + undilate(far_owned[:, 1].reshape(-1, head_count, head_size), far_mask)
    )
    grad_query = unnormalize(query_inverse, query_unit, grad_qn)
    grad_key = unnormalize(key_inverse, key_unit, grad_kn)
    grad_qkv = jnp.concatenate(
        [
            grad_query.reshape(token_rows, width),
            grad_key.reshape(token_rows, width),
            grad_value.reshape(token_rows, width),
        ],
        axis=1,
    ).astype(jnp.bfloat16)
    grad_inputs = jnp.dot(grad_qkv, qkv_weight, preferred_element_type=jnp.float32).astype(
        jnp.bfloat16
    )
    qkv_term = lax.dot_general(
        grad_qkv, inputs, (((0,), (0,)), ((), ())), preferred_element_type=jnp.float32
    )
    out_term = lax.dot_general(
        attn_flat, incoming, (((0,), (0,)), ((), ())), preferred_element_type=jnp.float32
    )
    qkv_share, out_share = (
        lax.psum_scatter(qkv_term, ("seq", "dp"), scatter_dimension=0, tiled=True),
        lax.psum_scatter(out_term, ("seq", "dp"), scatter_dimension=0, tiled=True),
    )
    return (branch[None], grad_inputs[None], qkv_share, out_share)


def solution(mesh):
    return jax.shard_map(
        body,
        mesh=mesh,
        in_specs=(P("dp", "seq", None), P("dp", "seq", None), P(), P(), P(), P(), P()),
        out_specs=(
            P("dp", "seq", None),
            P("dp", "seq", None),
            P(("seq", "dp"), None),
            P(("seq", "dp"), None),
        ),
        check_vma=False,
    )
```

profile of v0, /device:TPU:1, one launch (start us, length us, event | category | flops | bytes accessed | tf_op | source)
XLA Modules:
  0.0 692.2 jit_solution(18185178488744743185)
XLA Ops:
  7.2 1.9 copy-done
  9.2 2.2 convolution_convert_fusion
  12.4 1.9 copy.138
  14.3 2.2 reshape.238
  16.5 1.9 copy.139
  18.4 2.3 reshape.237
  24.6 2.6 convolution_convert_fusion.2
  27.2 2.1 reshape_reshape.14
  29.2 2.1 reshape_reshape.12
  33.5 3.1 select_reduce_fusion
  42.4 3.2 collective-permute-start
  45.6 1.7 copy.159
  47.4 1.7 copy.137
  49.1 2.4 reshape.240
  52.2 2.4 reshape.239
  56.5 1.9 reshape_reshape.15
  58.4 1.9 reshape_reshape.13
  60.2 5.9 fusion.39
  66.2 1.7 copy.153
  67.9 1.7 copy.152
  70.3 50.6 %all_gather.3 = bf16[128,2,768]{2,1,0:T(2,128)(2,1)S(1)} all-gather(bf16[2,2,768]{2,1,0:T(2,128)(2,1)S(1)} %pad_maximum_fusion.5), channel_id=1, replica_groups=mesh['seq'=64,'dp'=4] {'seq'}, dimensions={0}, use_global_device_ids=true | all-gather | bytes 399360 | tf_op jit(solution)/shard_map/all_gather | solution.py:144
  122.3 1.8 copy.156
  124.1 2.5 fusion.73
  126.6 1.8 copy.154
  129.9 1.7 convolution_bitcast_fusion.7
  141.1 1.7 copy.158
  142.7 2.6 broadcast_in_dim.295
  145.4 2.3 broadcast_in_dim.296
  150.8 2.0 collective-permute-start.2
  152.8 2.9 fusion.75
  155.7 6.6 collective-permute-done.2
  163.2 1.7 copy.145
  164.9 1.8 fusion.74
  169.0 1.7 copy.143
  172.9 2.2 copy.147
  177.0 3.0 multiply_reduce_fusion
  186.6 1.9 fusion.63
  194.9 1.9 copy.175
  196.8 1.9 copy.174
  198.7 2.7 pad_maximum_fusion.1
  201.5 2.3 select_convert_fusion.2
  205.5 2.7 broadcast_in_dim.307
  208.1 2.3 broadcast_in_dim.308
  210.4 1.9 broadcast_bitcast_fusion.2
  212.3 2.1 copy.163
  214.5 3.0 fusion.47
  217.9 6.5 collective-permute-done.3
  226.3 10.5 %collective-permute-done.4 = bf16[32,2,768]{0,2,1:T(8,128)(2,1)S(1)} collective-permute-done((bf16[32,2,768]{0,2,1:T(8,128)(2,1)S(1)}, bf16[32,2,768]{0,2,1:T(8,128)(2,1)S(1)}, u32[]{:S(2)}, u32[]{:S(2)}) %collective-permute-start.4) | collective-permute-done | bytes 98336 | tf_op jit(solution)/shard_map/ppermute | solution.py:20
  241.2 1.8 copy.178
  243.0 1.9 broadcast_bitcast_fusion
  244.9 2.2 copy.179
  247.0 1.8 copy.170
  248.8 1.9 broadcast_bitcast_fusion.1
  250.7 2.2 copy.171
  252.9 128.8 %all-reduce.7.cloned.1.call-done = f32[128,2,768]{2,1,0:T(2,128)} async-done(((f32[128,2,768]{2,1,0:T(2,128)}), f32[128,2,768]{2,1,0:T(2,128)}) %all-reduce.7.cloned.1.call-update) | async-done | bytes 786448
  384.7 2.6 broadcast_in_dim.319
  387.3 2.3 broadcast_in_dim.320
  389.7 1.7 copy.196
  391.3 2.6 broadcast_in_dim.313
  394.0 2.4 broadcast_in_dim.314
  396.4 1.9 fusion.12
  399.6 4.0 fusion.46
  403.6 2.5 fusion.24
  407.5 275.0 %all-reduce.9.cloned.1.call-done = (f32[2304,768]{1,0:T(8,128)}, f32[768,768]{1,0:T(8,128)}) async-done(((f32[2304,768]{1,0:T(8,128)}, f32[768,768]{1,0:T(8,128)}), (f32[2304,768]{1,0:T(8,128)}, f32[768,768]{1,0:T(8,128)})) %all-reduce.9.cloned.1.call-update) | async-done | bytes 9437200
  (160 shorter events, 68.1 us)
Async XLA Ops:
  7.2 2.0 copy-start
  7.2 374.5 %all-reduce.7.cloned.1.call-start = ((), (), s32[]{:S(2)}) async-start(), calls=%async_computation | async-start | bytes 1572864
  18.4 5.6 copy-start.42
  42.4 86.0 %collective-permute-start = (bf16[16,2,768]{2,0,1:T(8,128)(2,1)}, bf16[16,2,768]{2,0,1:T(8,128)(2,1)}, u32[]{:S(2)}, u32[]{:S(2)}) collective-permute-start(bf16[16,2,768]{2,0,1:T(8,128)(2,1)} %constant_dynamic-update-slice_fusion), channel_id=1, source_target_pairs={{0,4},{4,0},{8,12},{12,8},{16,20},{20,16},{24,28},{28,24},{32,36},... | collective-permute-start | bytes 147464 | tf_op jit(solution)/shard_map/ppermute | solution.py:20
  129.9 19.7 %collective-permute-start.1 = (bf16[32,2,768]{2,0,1:T(8,128)(2,1)}, bf16[32,2,768]{2,0,1:T(8,128)(2,1)}, u32[]{:S(2)}, u32[]{:S(2)}) collective-permute-start(bf16[32,2,768]{2,0,1:T(8,128)(2,1)} %maximum_select_fusion.2), channel_id=1, source_target_pairs={{0,8},{8,0},{4,12},{12,4},{16,24},{24,16},{20,28},{28,20},{32,40},... | collective-permute-start | bytes 294920 | tf_op jit(solution)/shard_map/ppermute | solution.py:20
  150.8 11.5 %collective-permute-start.2 = (bf16[64,2,768]{2,0,1:T(8,128)(2,1)S(1)}, bf16[64,2,768]{2,0,1:T(8,128)(2,1)S(1)}, u32[]{:S(2)}, u32[]{:S(2)}) collective-permute-start(bf16[64,2,768]{2,0,1:T(8,128)(2,1)S(1)} %maximum_select_fusion.1), channel_id=1, source_target_pairs={{0,16},{16,0},{4,20},{20,4},{8,24},{24,8},{12,28},{28,12},{32,48},... | collective-permute-start | bytes 589832 | tf_op jit(solution)/shard_map/ppermute | solution.py:20
  185.7 4.2 copy-start.20
  185.7 5.1 copy-start.11
  185.7 5.9 copy-start.29
  185.7 5.9 copy-start.30
  185.7 5.9 copy-start.39
  185.7 6.1 copy-start.25
  185.7 6.1 copy-start.31
  188.5 4.3 copy-start.27
  188.5 4.3 copy-start.40
  188.5 4.5 copy-start.28
  189.8 4.3 copy-start.16
  201.5 481.0 %all-reduce.9.cloned.1.call-start = ((), (), s32[]{:S(2)}) async-start(), calls=%async_computation.1 | async-start | bytes 18874368
  203.8 20.6 %collective-permute-start.3 = (bf16[64,2,768]{0,2,1:T(8,128)(2,1)}, bf16[64,2,768]{0,2,1:T(8,128)(2,1)}, u32[]{:S(2)}, u32[]{:S(2)}) collective-permute-start(bf16[64,2,768]{0,2,1:T(8,128)(2,1)} %select_convert_fusion.2), channel_id=1, source_target_pairs={{0,16},{16,0},{4,20},{20,4},{8,24},{24,8},{12,28},{28,12},{32,48},... | collective-permute-start | bytes 589832 | tf_op jit(solution)/shard_map/ppermute | solution.py:20
  214.4 3.0 copy-start.4
  214.4 3.0 copy-start.9
  214.4 3.0 copy-start.17
  214.4 3.0 copy-start.32
  214.4 3.0 copy-start.34
  214.5 3.0 copy-start.41
  217.4 7.0 %copy-start.6 = (f32[12,64,128]{2,1,0:T(8,128)S(1)}, f32[12,64,128]{2,1,0:T(8,128)}, u32[]{:S(2)}) copy-start(f32[12,64,128]{2,1,0:T(8,128)} %fusion.54) | copy-start | bytes 1179652
  217.4 7.0 %copy-start.7 = (f32[12,64,128]{2,1,0:T(8,128)S(1)}, f32[12,64,128]{2,1,0:T(8,128)}, u32[]{:S(2)}) copy-start(f32[12,64,128]{2,1,0:T(8,128)} %fusion.59) | copy-start | bytes 1179652
  217.8 8.2 %copy-start.8 = (bf16[12,128,128]{1,2,0:T(8,128)(2,1)}, bf16[12,128,128]{1,2,0:T(8,128)(2,1)S(1)}, u32[]{:S(2)}) copy-start(bf16[12,128,128]{1,2,0:T(8,128)(2,1)S(1)} %fusion.4) | copy-start | bytes 1179652
  217.8 8.2 %copy-start.1 = (f32[128,768]{0,1:T(8,128)S(1)}, f32[128,768]{0,1:T(8,128)}, u32[]{:S(2)}) copy-start(f32[128,768]{0,1:T(8,128)} %copy.139) | copy-start | bytes 1179652
  217.8 8.2 %copy-start.22 = (f32[128,12,64]{0,2,1:T(8,128)S(1)}, f32[128,12,64]{0,2,1:T(8,128)}, u32[]{:S(2)}) copy-start(f32[128,12,64]{0,2,1:T(8,128)} %broadcast_in_dim.308) | copy-start | bytes 1179652
  217.9 8.2 %copy-start.24 = (f32[128,12,64]{0,2,1:T(8,128)S(1)}, f32[128,12,64]{0,2,1:T(8,128)}, u32[]{:S(2)}) copy-start(f32[128,12,64]{0,2,1:T(8,128)} %copy.163) | copy-start | bytes 1179652
  217.9 8.2 %copy-start.35 = (pred[128,12]{0,1:T(8,128)(4,1)S(1)}, pred[128,12]{0,1:T(8,128)(4,1)}, u32[]{:S(2)}) copy-start(pred[128,12]{0,1:T(8,128)(4,1)} %broadcast_in_dim.291) | copy-start | bytes 4612
  217.9 8.2 %copy-start.37 = (pred[128,12]{0,1:T(8,128)(4,1)S(1)}, pred[128,12]{0,1:T(8,128)(4,1)}, u32[]{:S(2)}) copy-start(pred[128,12]{0,1:T(8,128)(4,1)} %broadcast_in_dim.283) | copy-start | bytes 4612
  225.9 10.9 %collective-permute-start.4 = (bf16[32,2,768]{0,2,1:T(8,128)(2,1)S(1)}, bf16[32,2,768]{0,2,1:T(8,128)(2,1)S(1)}, u32[]{:S(2)}, u32[]{:S(2)}) collective-permute-start(bf16[32,2,768]{0,2,1:T(8,128)(2,1)S(1)} %select_convert_fusion.1), channel_id=1, source_target_pairs={{0,8},{8,0},{4,12},{12,4},{16,24},{24,16},{20,28},{28,20},{32,40},... | collective-permute-start | bytes 294920 | tf_op jit(solution)/shard_map/ppermute | solution.py:20
  237.0 1.6 copy-start.3
  237.2 2.8 collective-permute-start.5
  396.3 1.9 copy-start.2
  396.3 2.1 copy-start.5
  396.3 2.1 copy-start.10
  396.3 2.1 copy-start.21
  396.3 2.1 copy-start.23
  396.3 2.1 copy-start.33
  396.4 2.1 copy-start.36
  396.4 2.1 copy-start.38
  398.5 0.7 copy-start.14
  398.5 1.1 copy-start.12
  398.5 1.1 copy-start.26
  398.9 0.7 copy-start.18
  403.6 2.5 copy-start.13
  403.6 2.5 copy-start.15
  403.6 2.5 copy-start.19
Sparse Core Ops, SparseCore 0:
  201.6 180.0 all-reduce.6
  403.7 278.7 all-reduce.8
where the time goes:
time: 696 us; the launch traced here: 692 us
  waiting for transfers between devices  428 us (61%)
  local copies, waits for them, and re-layouts  122 us (18%)
  blocking collectives  50.6 us (7%)
  matrix products  39.6 us (6%)
  other arithmetic  30.3 us (4%)
  between operations  15.3 us (2%)
    unnamed x4, waiting for transfers between devices  404 us
    broadcast_in_dim x28, local copies, waits for them, and re-layouts, undilate(): spread = jnp.where(pick[None], values[:, None], jnp.zeros((), values.dtype))  52.5 us
    all_gather x1, blocking collectives, body(): lax.all_gather(pack_rows(dilate(key_norm, far_mask), dilate(value, far_ma...  50.6 us
    ppermute x6, waiting for transfers between devices, from_partner(): return lax.ppermute(block, axis, route)  24.1 us
  transfers between devices with their start and end apart: 8, of which 6 were waited for; matrix products, arithmetic and copies ran while one was open for 13% of the time, Pallas kernels for 0%

commit v1 on v0

v1 whole, which is shorter than its diff:
```python
import jax
import jax.numpy as jnp
import numpy as np
from jax import lax
from jax.experimental import pallas as pl
from jax.experimental.pallas import tpu as pltpu
from jax.sharding import PartitionSpec as P

BF = jnp.bfloat16
F32 = jnp.float32
MESH = pl.DeviceIdType.MESH
EPS = 1e-06

NY, NZ, NX = 4, 8, 4
TOK = 128
WIDTH = 768
HEADS = 12
HEAD = 64
GROUP = 4
LANES = GROUP * HEAD
GROUPS = HEADS // GROUP
SPAN = 8
NEAR = TOK // SPAN
FAR = 2
PACK = 4 * FAR * WIDTH // 128
HALF = WIDTH // 2
QROWS = 3 * WIDTH // NY
OROWS = WIDTH // NY
PIECE = QROWS + OROWS
QZ, OZ = QROWS // NZ, OROWS // NZ
ZROWS = QZ + OZ


def nn(a, b):
    return lax.dot_general(a, b, (((1,), (0,)), ((), ())), preferred_element_type=F32)


def nt(a, b):
    return lax.dot_general(a, b, (((1,), (1,)), ((), ())), preferred_element_type=F32)


def tn(a, b):
    return lax.dot_general(a, b, (((0,), (0,)), ((), ())), preferred_element_type=F32)


def split(x):
    high = x.astype(BF)
    return high, (x - high.astype(F32)).astype(BF)


def iota(shape, dim):
    return lax.broadcasted_iota(jnp.int32, shape, dim)


def place():
    seq = lax.axis_index("seq")
    return seq, lax.rem(seq, 2), lax.rem(seq // 2, NZ), seq // (2 * NZ)


def at(y, z, core):
    return {"seq": (y * NZ + z) * 2 + core}


def remote(src, dst, send, recv, device):
    return pltpu.make_async_remote_copy(
        src_ref=src, dst_ref=dst, send_sem=send, recv_sem=recv, device_id=device, device_id_type=MESH
    )


def greet(devices):
    barrier = pltpu.get_barrier_semaphore()
    for device in devices:
        pl.semaphore_signal(barrier, inc=1, device_id=device, device_id_type=MESH)
    pl.semaphore_wait(barrier, len(devices))


def lanes_of(b):
    return slice(b * LANES, (b + 1) * LANES)


def attention(
    scale_ref, near_ref, far_ref, tok_ref, cot_ref, wqkv_ref, wout_ref, block_ref, compact_ref, order_ref,
    branch_ref, attn_ref, dqkv_ref,
    qkv, qn, kn, gr, inv_q, inv_k, p_loc, p_near, p_far, num, den, dq, dk, dv, pack,
    near_kv, near_qg, near_s, far_z, far_kv, far_qg, far_sz, far_s,
    s_nkv, r_nkv, s_nqg, r_nqg, s_ns, r_ns, s_fz, r_fz, s_fsz, r_fsz,
    s_fkv, r_fkv, s_fqg, r_fqg, s_fs, r_fs, s_ckv, r_ckv, s_cqg, r_cqg, s_cs, r_cs,
):
    seq, core, z, y = place()
    mine = lax.rem(seq, SPAN)
    base = seq - mine
    other = 1 - core
    near_peers = [lax.rem(mine + d, SPAN) for d in range(1, SPAN)]
    z_peers = [lax.rem(z + d, NZ) for d in range(1, NZ)]
    y_peers = [lax.rem(y + d, NY) for d in range(1, NY)]
    quad = mine // 2
    greet(
        [at(y, t, core) for t in z_peers]
        + [{"seq": base + 2 * lax.rem(quad + d, SPAN // 2) + other} for d in range(SPAN // 2)]
        + [at(t, z, core) for t in y_peers]
    )
    sent = []

    def send(src, dst, ssem, rsem, device):
        copy = remote(src, dst, ssem, rsem, device)
        copy.start()
        sent.append(copy)

    def arrived(ref, ssem, rsem):
        remote(ref, ref, ssem, rsem, {"seq": seq}).wait_recv()

    head_lane = iota((1, LANES), 1) // HEAD
    picks_f = [(head_lane == h).astype(F32) for h in range(GROUP)]
    picks = [m.astype(BF) for m in picks_f]

    def spread(x):
        return jnp.concatenate([x * m for m in picks], axis=0)

    def fold(x):
        rows = x.shape[0] // GROUP
        return sum(x[h * rows : (h + 1) * rows] * picks_f[h] for h in range(GROUP))

    def norms(columns):
        wide = columns.astype(F32)
        high, low = split(wide * wide)
        inverse = lax.rsqrt(nn(high, block_ref[...]) + nn(low, block_ref[...]) + EPS)
        return inverse, wide * inverse

    tok = tok_ref[...]
    cot = cot_ref[...]
    for b in range(3 * GROUPS):
        qkv[:, lanes_of(b)] = nt(tok, wqkv_ref[lanes_of(b), :]).astype(BF)
    for b in range(GROUPS):
        gr[:, lanes_of(b)] = nt(cot, wout_ref[lanes_of(b), :]).astype(BF)
        inverse, unit = norms(qkv[:, lanes_of(b)])
        inv_q[:, lanes_of(b)] = inverse
        qn[:, lanes_of(b)] = unit.astype(BF)
        inverse, unit = norms(qkv[:, lanes_of(GROUPS + b)])
        inv_k[:, lanes_of(b)] = inverse
        kn[:, lanes_of(b)] = unit.astype(BF)

    wide_head = iota((1, WIDTH), 1) // HEAD
    slim_head = iota((1, 128), 1)
    slim_head = jnp.where(slim_head >= HEADS, slim_head - HEADS, slim_head)
    near_row, far_row = jnp.zeros((1, WIDTH), jnp.int32), jnp.zeros((1, WIDTH), jnp.int32)
    near_slim, far_slim = jnp.zeros((1, 128), jnp.int32), jnp.zeros((1, 128), jnp.int32)
    for h in range(HEADS):
        near_row = jnp.where(wide_head == h, near_ref[h], near_row)
        far_row = jnp.where(wide_head == h, far_ref[h], far_row)
        near_slim = jnp.where(slim_head == h, near_ref[h], near_slim)
        far_slim = jnp.where(slim_head == h, far_ref[h], far_slim)
    near_mask = ((iota((TOK, WIDTH), 0) & (SPAN - 1)) == near_row).astype(F32)
    far_mask = ((iota((TOK, WIDTH), 0) & (TOK // FAR - 1)) == far_row).astype(F32)
    near_bf, far_bf = near_mask.astype(BF), far_mask.astype(BF)
    near_slim = ((iota((TOK, 128), 0) & (SPAN - 1)) == near_slim).astype(F32).astype(BF)
    far_slim = ((iota((TOK, 128), 0) & (TOK // FAR - 1)) == far_slim).astype(F32).astype(BF)
    row, token = iota((NEAR, TOK), 0), iota((NEAR, TOK), 1)
    take_near = (token // SPAN == row).astype(F32).astype(BF)
    take_far = (token // (TOK // FAR) == row).astype(F32).astype(BF)
    take_far_z = ((row // FAR == z) & (token // (TOK // FAR) == (row & 1))).astype(F32).astype(BF)

    def unnear(x, b):
        return jnp.broadcast_to(x[:, None, :], (NEAR, SPAN, LANES)).reshape(TOK, LANES) * near_mask[:, lanes_of(b)]

    def unfar(x, b):
        rows = [jnp.broadcast_to(x[i : i + 1], (TOK // FAR, LANES)) for i in range(FAR)]
        return jnp.concatenate(rows, axis=0) * far_mask[:, lanes_of(b)]

    value = qkv[:, 2 * WIDTH :]
    rows = [kn[...], value, qn[...], gr[...]]
    far_rows = []
    for i, x in enumerate(rows):
        into = near_kv if i < 2 else near_qg
        into[mine, i % 2] = nn(take_near, x * near_bf).astype(BF)
        picked = nn(take_far, x * far_bf)
        far_rows.append(picked.astype(BF))
        for r in range(FAR):
            for t in range(WIDTH // 128):
                at_row = (i * FAR + r) * (WIDTH // 128) + t
                pack[at_row : at_row + 1, :] = picked[r : r + 1, 128 * t : 128 * (t + 1)]
    far_z[z] = pack[...].astype(BF)
    for n, t in enumerate(z_peers):
        send(far_z.at[z], far_z.at[z], s_fz.at[n], r_fz.at[z], at(y, t, core))
    for n, t in enumerate(near_peers):
        send(near_kv.at[mine], near_kv.at[mine], s_nkv.at[n], r_nkv.at[mine], {"seq": base + t})
    for n, t in enumerate(near_peers):
        send(near_qg.at[mine], near_qg.at[mine], s_nqg.at[n], r_nqg.at[mine], {"seq": base + t})

    ones = spread(jnp.ones((TOK, LANES), BF))
    for b in range(GROUPS):
        s = nt(spread(qn[:, lanes_of(b)]), kn[:, lanes_of(b)])
        ps = []
        for h in range(GROUP):
            p = jnp.exp(s[h * TOK : (h + 1) * TOK] * scale_ref[GROUP * b + h])
            p_loc[(GROUP * b + h) * TOK : (GROUP * b + h + 1) * TOK, :] = p
            ps.append(p.astype(BF))
        ps = jnp.concatenate(ps, axis=1)
        num[:, lanes_of(b)] = nn(ps, spread(qkv[:, lanes_of(2 * GROUPS + b)]))
        den[:, lanes_of(b)] = nn(ps, ones)

    for t in z_peers:
        arrived(far_z.at[t], s_fz.at[0], r_fz.at[t])
    ordered = nn(order_ref[...], far_z[...].reshape(NZ * PACK, 128)).astype(BF)
    for i in range(4):
        into = far_kv if i < 2 else far_qg
        for t in range(WIDTH // 128):
            first = (i * (WIDTH // 128) + t) * 16
            into[core, y, i % 2, :, 128 * t : 128 * (t + 1)] = ordered[first : first + 16, :]
    for n, t in enumerate(y_peers):
        send(far_kv.at[core, y], far_kv.at[core, y], s_fkv.at[n], r_fkv.at[y], at(t, z, core))
    for n, t in enumerate(y_peers):
        send(far_qg.at[core, y], far_qg.at[core, y], s_fqg.at[n], r_fqg.at[y], at(t, z, core))

    def forward(queries, keys, values, p_ref):
        results = []
        for b in range(GROUPS):
            s = nt(spread(queries[:, lanes_of(b)]), keys(b))
            ps = []
            for h in range(GROUP):
                ps.append(jnp.exp(s[h * 16 : (h + 1) * 16] * scale_ref[GROUP * b + h]))
            p = jnp.concatenate(ps, axis=0)
            p_ref[b] = p
            total = jnp.broadcast_to(jnp.sum(p, axis=1, keepdims=True), (GROUP * 16, LANES))
            results.append((fold(nn(p.astype(BF), values(b))), fold(total)))
        return results

    def near_rows(ref, i):
        return lambda b: jnp.concatenate([ref[s, i, :, lanes_of(b)] for s in range(SPAN)], axis=0)

    def far_rows_of(ref, i):
        return lambda b: jnp.concatenate(
            [ref[s, t, i, :, lanes_of(b)] for s in range(2) for t in range(NY)], axis=0
        )

    for t in near_peers:
        arrived(near_kv.at[t], s_nkv.at[0], r_nkv.at[t])
    near_q, near_g = near_qg[mine, 0], near_qg[mine, 1]
    for b, (n_part, d_part) in enumerate(forward(near_q, near_rows(near_kv, 0), near_rows(near_kv, 1), p_near)):
        num[:, lanes_of(b)] += unnear(n_part, b)
        den[:, lanes_of(b)] += unnear(d_part, b)

    partner = at(y, z, other)
    for t in y_peers:
        arrived(far_kv.at[core, t], s_fkv.at[0], r_fkv.at[t])
    send(far_kv.at[core], far_kv.at[core], s_ckv, r_ckv, partner)
    for t in y_peers:
        arrived(far_qg.at[core, t], s_fqg.at[0], r_fqg.at[t])
    send(far_qg.at[core], far_qg.at[core], s_cqg, r_cqg, partner)
    arrived(far_kv.at[other], s_ckv, r_ckv)
    far_k, far_v, far_q, far_g = far_rows
    for b, (n_part, d_part) in enumerate(forward(far_q, far_rows_of(far_kv, 0), far_rows_of(far_kv, 1), p_far)):
        num[:, lanes_of(b)] += unfar(n_part, b)
        den[:, lanes_of(b)] += unfar(d_part, b)

    inverse = 1.0 / den[...]
    attn = (num[...] * inverse).astype(BF)
    attn_ref[...] = attn
    high, low = split(inverse)
    slim = nn(high, compact_ref[:, :128]) + nn(low, compact_ref[:, :128])
    high, low = split(gr[...].astype(F32) * attn.astype(F32))
    slim = slim + nn(high, compact_ref[:, 128:]) + nn(low, compact_ref[:, 128:])
    high, low = split(slim)

    def take(selection, mask):
        return nn(selection, high * mask) + nn(selection, low * mask)

    near_slim_rows = take(take_near, near_slim)
    far_slim_rows = take(take_far, far_slim)
    near_s[mine] = near_slim_rows
    far_sz[z] = take(take_far_z, far_slim)
    for n, t in enumerate(z_peers):
        send(far_sz.at[z], far_sz.at[z], s_fsz.at[n], r_fsz.at[z], at(y, t, core))
    for n, t in enumerate(near_peers):
        send(near_s.at[mine], near_s.at[mine], s_ns.at[n], r_ns.at[mine], {"seq": base + t})
    branch_ref[...] = nn(attn, wout_ref[...]).astype(BF)

    for b in range(GROUPS):
        g = spread(gr[:, lanes_of(b)])
        grad_p = nt(g, qkv[:, lanes_of(2 * GROUPS + b)])
        ps, ds = [], []
        for h in range(GROUP):
            n = GROUP * b + h
            p = p_loc[n * TOK : (n + 1) * TOK, :] * slim[:, n : n + 1]
            d = scale_ref[n] * p * (grad_p[h * TOK : (h + 1) * TOK] - slim[:, HEADS + n : HEADS + n + 1])
            ps.append(p.astype(BF))
            ds.append(d.astype(BF))
        dq[:, lanes_of(b)] = nn(jnp.concatenate(ds, axis=1), spread(kn[:, lanes_of(b)]))
        dk[:, lanes_of(b)] = tn(jnp.concatenate(ds, axis=0), spread(qn[:, lanes_of(b)]))
        dv[:, lanes_of(b)] = tn(jnp.concatenate(ps, axis=0), g)

    for t in z_peers:
        arrived(far_sz.at[t], s_fsz.at[0], r_fsz.at[t])
    far_s[core, y] = jnp.sum(far_sz[...], axis=0)
    for n, t in enumerate(y_peers):
        send(far_s.at[core, y], far_s.at[core, y], s_fs.at[n], r_fs.at[y], at(t, z, core))

    def query_side(grads, keys, values, p_ref, slim_rows, b):
        grad_p = nt(spread(grads[:, lanes_of(b)]), values(b))
        ds = []
        for h in range(GROUP):
            n = GROUP * b + h
            p = p_ref[b, h * 16 : (h + 1) * 16, :] * slim_rows[:, n : n + 1]
            ds.append(
                scale_ref[n] * p * (grad_p[h * 16 : (h + 1) * 16] - slim_rows[:, HEADS + n : HEADS + n + 1])
            )
        return fold(nn(jnp.concatenate(ds, axis=0).astype(BF), keys(b)))

    for b in range(GROUPS):
        near_part = query_side(near_g, near_rows(near_kv, 0), near_rows(near_kv, 1), p_near, near_slim_rows, b)
        far_part = query_side(far_g, far_rows_of(far_kv, 0), far_rows_of(far_kv, 1), p_far, far_slim_rows, b)
        dq[:, lanes_of(b)] += unnear(near_part, b) + unfar(far_part, b)

    for t in y_peers:
        arrived(far_s.at[core, t], s_fs.at[0], r_fs.at[t])
    send(far_s.at[core], far_s.at[core], s_cs, r_cs, partner)

    def key_side(keys, values, queries, grads, columns, b):
        q, g = queries(b), grads(b)
        s = nt(spread(keys[:, lanes_of(b)]), q)
        grad_p = nt(spread(values[:, lanes_of(b)]), g)
        ps, ds = [], []
        for h in range(GROUP):
            n = GROUP * b + h
            p = jnp.exp(s[h * 16 : (h + 1) * 16] * scale_ref[n]) * columns[n : n + 1, :]
            ps.append(p)
            ds.append(
                scale_ref[n] * p * (grad_p[h * 16 : (h + 1) * 16] - columns[HEADS + n : HEADS + n + 1, :])
            )
        p, d = jnp.concatenate(ps, axis=0).astype(BF), jnp.concatenate(ds, axis=0).astype(BF)
        return fold(nn(d, q)), fold(nn(p, g))

    for t in near_peers:
        arrived(near_s.at[t], s_ns.at[0], r_ns.at[t])
        arrived(near_qg.at[t], s_nqg.at[0], r_nqg.at[t])
    columns = near_s[...].reshape(TOK, 128).T
    near_k, near_v = near_kv[mine, 0], near_kv[mine, 1]
    for b in range(GROUPS):
        k_part, v_part = key_side(near_k, near_v, near_rows(near_qg, 0), near_rows(near_qg, 1), columns, b)
        dk[:, lanes_of(b)] += unnear(k_part, b)
        dv[:, lanes_of(b)] += unnear(v_part, b)
    arrived(far_qg.at[other], s_cqg, r_cqg)
    arrived(far_s.at[other], s_cs, r_cs)
    columns = far_s[...].reshape(TOK, 128).T
    for b in range(GROUPS):
        k_part, v_part = key_side(far_k, far_v, far_rows_of(far_qg, 0), far_rows_of(far_qg, 1), columns, b)
        dk[:, lanes_of(b)] += unfar(k_part, b)
        dv[:, lanes_of(b)] += unfar(v_part, b)

    for i, (inv_ref, grad) in enumerate(((inv_q, dq), (inv_k, dk))):
        for b in range(GROUPS):
            inverse = inv_ref[:, lanes_of(b)]
            unit = qkv[:, lanes_of(GROUPS * i + b)].astype(F32) * inverse
            d = grad[:, lanes_of(b)]
            high, low = split(unit * d)
            along = nn(high, block_ref[...]) + nn(low, block_ref[...])
            dqkv_ref[:, lanes_of(GROUPS * i + b)] = (inverse * (d - unit * along)).astype(BF)
    dqkv_ref[:, 2 * WIDTH :] = dv[...].astype(BF)
    for copy in sent:
        copy.wait_send()


def weights(
    dqkv_ref, tok_ref, attn_ref, cot_ref, wqkv_ref, deal_ref,
    grad_tok_ref, qkv_out, out_out,
    dqkv_t, attn_t, part, total, core_send, core_recv, y_send, y_recv, z_send, z_recv, x_pieces,
    s_core, r_core, s_y, r_y, s_z, r_z, s_x, r_x,
):
    seq, core, z, y = place()
    x = lax.axis_index("dp")
    other = 1 - core
    partner = at(y, z, other)
    y_right, y_left = at(lax.rem(y + 1, NY), z, core), at(lax.rem(y + 3, NY), z, core)
    z_right, z_left = at(y, lax.rem(z + 1, NZ), core), at(y, lax.rem(z + NZ - 1, NZ), core)
    pair = seq - core
    owners = []
    for d in range(1, 2 * NX):
        to = lax.rem(core * NX + x + d, 2 * NX)
        owners.append((to, {"seq": pair + to // NX, "dp": lax.rem(to, NX)}))
    greet([partner_ for partner_ in (y_right, y_left, z_right, z_left)] + [device for _, device in owners])
    sent = []

    def send(src, dst, ssem, rsem, device):
        copy = remote(src, dst, ssem, rsem, device)
        copy.start()
        sent.append(copy)

    def arrived(ref, ssem, rsem):
        remote(ref, ref, ssem, rsem, {"seq": seq}).wait_recv()

    tok, cot = tok_ref[...], cot_ref[...]
    first = core == 0
    tok_mine = jnp.where(first, tok[:, :HALF], tok[:, HALF:])
    tok_other = jnp.where(first, tok[:, HALF:], tok[:, :HALF])
    cot_mine = jnp.where(first, cot[:, :HALF], cot[:, HALF:])
    cot_other = jnp.where(first, cot[:, HALF:], cot[:, :HALF])
    dqkv_t[...] = dqkv_ref[...].T
    attn_t[...] = attn_ref[...].T

    turns = (2, 1, 3, 0)
    for n, turn in enumerate(turns):
        p = lax.rem(y + turn, NY)
        q_rows = pl.ds(pl.multiple_of(p * QROWS, 64), QROWS)
        o_rows = pl.ds(pl.multiple_of(p * OROWS, 64), OROWS)
        core_send[n, :QROWS, :] = nn(dqkv_t[q_rows, :], tok_other).astype(BF)
        core_send[n, QROWS:, :] = nn(attn_t[o_rows, :], cot_other).astype(BF)
        send(core_send.at[n], core_recv.at[n], s_core.at[n], r_core.at[n], partner)
        part[n, :QROWS, :] = nn(dqkv_t[q_rows, :], tok_mine)
        part[n, QROWS:, :] = nn(attn_t[o_rows, :], cot_mine)

    grad_tok_ref[...] = nn(dqkv_ref[...], wqkv_ref[...]).astype(BF)

    a, b = slice(0, PIECE // 2), slice(PIECE // 2, PIECE)

    def both_cores(n):
        arrived(core_recv.at[n], s_core.at[n], r_core.at[n])
        part[n] += core_recv[n].astype(F32)

    def y_out(slot, value, device, into=None):
        y_send[slot] = value.astype(BF)
        send(y_send.at[slot], y_recv.at[slot], s_y.at[slot], r_y.at[slot], device)

    def y_in(slot):
        arrived(y_recv.at[slot], s_y.at[slot], r_y.at[slot])
        return y_recv[slot].astype(F32)

    both_cores(0)
    y_out(0, part[0, a, :], y_right)
    y_out(1, part[0, b, :], y_left)
    both_cores(1)
    y_out(2, part[1, b, :], y_right)
    both_cores(2)
    y_out(4, part[2, a, :], y_left)
    y_out(3, part[1, a, :] + y_in(0), y_right)
    y_out(5, part[2, b, :] + y_in(1), y_left)
    both_cores(3)
    total[b, :] = part[3, b, :] + y_in(2)
    total[a, :] = part[3, a, :] + y_in(4)
    total[a, :] += y_in(3)
    total[b, :] += y_in(5)

    def block(t):
        q_rows = pl.ds(pl.multiple_of(t * QZ, 8), QZ)
        o_rows = pl.ds(pl.multiple_of(QROWS + t * OZ, 8), OZ)
        return jnp.concatenate([total[q_rows, :], total[o_rows, :]], axis=0)

    half = ZROWS // 2
    slices = (slice(0, half), slice(half, ZROWS))

    def z_out(side, step, value, rows):
        z_send[side, step, rows, :] = value.astype(BF)
        send(
            z_send.at[side, step, rows], z_recv.at[side, step, rows], s_z.at[side, step], r_z.at[side, step],
            (z_right, z_left)[side],
        )

    def z_in(side, step, rows):
        arrived(z_recv.at[side, step, rows], s_z.at[side, step], r_z.at[side, step])
        return z_recv[side, step, rows, :].astype(F32)

    far = block(lax.rem(z + NZ // 2, NZ))
    for side in range(2):
        z_out(side, 0, far[slices[side]], slices[side])
    whole = slice(0, ZROWS)
    for step in range(1, NZ // 2):
        for side in range(2):
            away = NZ // 2 - step
            here = block(lax.rem(z + (away if side == 0 else NZ - away), NZ))
            if step == 1:
                came = z_in(side, 0, slices[side])
                if side == 0:
                    here = jnp.concatenate([here[:half] + came, here[half:]], axis=0)
                else:
                    here = jnp.concatenate([here[:half], here[half:] + came], axis=0)
            else:
                here = here + z_in(side, step - 1, whole)
            z_out(side, step, here, whole)
    here = block(z) + z_in(0, NZ // 2 - 1, whole) + z_in(1, NZ // 2 - 1, whole)

    dealt = nn(deal_ref[...], here.astype(BF)).astype(BF)
    slot = core * NX + x
    for to in range(2 * NX):
        x_pieces[0, to] = dealt[16 * to : 16 * (to + 1), :]
    x_pieces[1, slot] = x_pieces[0, slot]
    for n, (to, device) in enumerate(owners):
        send(x_pieces.at[0, to], x_pieces.at[1, slot], s_x.at[n], r_x.at[slot], device)
    for to, _ in owners:
        arrived(x_pieces.at[1, to], s_x.at[0], r_x.at[to])
    for side in range(2):
        share = sum(x_pieces[1, side * NX + t].astype(F32) for t in range(NX))
        qkv_out[:, side * HALF : (side + 1) * HALF] = share[:9]
        out_out[:, side * HALF : (side + 1) * HALF] = share[9:12]
    for copy in sent:
        copy.wait_send()


def constants():
    lane = np.arange(WIDTH)
    block = (lane[:LANES, None] // HEAD == lane[None, :LANES] // HEAD).astype(np.float32)
    compact = np.zeros((WIDTH, 256), np.float32)
    compact[np.arange(HEADS) * HEAD, np.arange(HEADS)] = 1
    compact[lane, 128 + HEADS + lane // HEAD] = 1
    order = np.zeros((NZ * PACK, NZ * PACK), np.float32)
    tiles = WIDTH // 128
    for t in range(4):
        for j in range(tiles):
            for s in range(NZ):
                for i in range(FAR):
                    order[(t * tiles + j) * 16 + s * FAR + i, s * PACK + (t * FAR + i) * tiles + j] = 1
    deal = np.zeros((2 * NX * 16, ZROWS), np.float32)
    for core in range(2):
        for x in range(NX):
            for i in range(9):
                deal[(core * NX + x) * 16 + i, (core * NX + x) * 9 + i] = 1
            for i in range(3):
                deal[(core * NX + x) * 16 + 9 + i, QZ + (core * NX + x) * 3 + i] = 1
    return [jnp.asarray(m, BF) for m in (block, compact, order, deal)]


def body(tokens, cotangent, qkv_weight, out_weight, logit_scale, near_offsets, far_offsets):
    inputs, incoming = tokens[0], cotangent[0]
    block, compact, order, deal = constants()
    smem = pl.BlockSpec(memory_space=pltpu.SMEM)
    vmem = pl.BlockSpec(memory_space=pltpu.VMEM)
    dma = pltpu.SemaphoreType.DMA
    wide_bf = pltpu.VMEM((TOK, WIDTH), BF)
    wide = pltpu.VMEM((TOK, WIDTH), F32)
    branch, attn, dqkv = pl.pallas_call(
        attention,
        out_shape=[
            jax.ShapeDtypeStruct((TOK, WIDTH), BF),
            jax.ShapeDtypeStruct((TOK, WIDTH), BF),
            jax.ShapeDtypeStruct((TOK, 3 * WIDTH), BF),
        ],
        in_specs=[smem] * 3 + [vmem] * 7,
        out_specs=[vmem] * 3,
        scratch_shapes=[
            pltpu.VMEM((TOK, 3 * WIDTH), BF), wide_bf, wide_bf, wide_bf, wide, wide,
            pltpu.VMEM((HEADS * TOK, 128), F32),
            pltpu.VMEM((GROUPS, GROUP * 16, 128), F32),
            pltpu.VMEM((GROUPS, GROUP * 16, 128), F32),
            wide, wide, wide, wide, wide,
            pltpu.VMEM((PACK, 128), F32),
            pltpu.VMEM((SPAN, 2, NEAR, WIDTH), BF),
            pltpu.VMEM((SPAN, 2, NEAR, WIDTH), BF),
            pltpu.VMEM((SPAN, NEAR, 128), F32),
            pltpu.VMEM((NZ, PACK, 128), BF),
            pltpu.VMEM((2, NY, 2, 16, WIDTH), BF),
            pltpu.VMEM((2, NY, 2, 16, WIDTH), BF),
            pltpu.VMEM((NZ, 16, 128), F32),
            pltpu.VMEM((2, NY, 16, 128), F32),
            dma((7,)), dma((8,)), dma((7,)), dma((8,)), dma((7,)), dma((8,)),
            dma((7,)), dma((8,)), dma((7,)), dma((8,)),
            dma((3,)), dma((4,)), dma((3,)), dma((4,)), dma((3,)), dma((4,)),
            dma, dma, dma, dma, dma, dma,
        ],
        compiler_params=pltpu.CompilerParams(
            collective_id=0, has_side_effects=True, vmem_limit_bytes=48 * 1024 * 1024
        ),
    )(logit_scale, near_offsets, far_offsets, inputs, incoming, qkv_weight, out_weight, block, compact, order)
    grad_inputs, qkv_share, out_share = pl.pallas_call(
        weights,
        out_shape=[
            jax.ShapeDtypeStruct((TOK, WIDTH), BF),
            jax.ShapeDtypeStruct((9, WIDTH), F32),
            jax.ShapeDtypeStruct((3, WIDTH), F32),
        ],
        in_specs=[vmem] * 6,
        out_specs=[vmem] * 3,
        scratch_shapes=[
            pltpu.VMEM((3 * WIDTH, TOK), BF),
            pltpu.VMEM((WIDTH, TOK), BF),
            pltpu.VMEM((NY, PIECE, HALF), F32),
            pltpu.VMEM((PIECE, HALF), F32),
            pltpu.VMEM((NY, PIECE, HALF), BF),
            pltpu.VMEM((NY, PIECE, HALF), BF),
            pltpu.VMEM((6, PIECE // 2, HALF), BF),
            pltpu.VMEM((6, PIECE // 2, HALF), BF),
            pltpu.VMEM((2, NZ // 2, ZROWS, HALF), BF),
            pltpu.VMEM((2, NZ // 2, ZROWS, HALF), BF),
            pltpu.VMEM((2, 2 * NX, 16, HALF), BF),
            dma((4,)), dma((4,)), dma((6,)), dma((6,)), dma((2, 4)), dma((2, 4)), dma((7,)), dma((8,)),
        ],
        compiler_params=pltpu.CompilerParams(
            collective_id=1, has_side_effects=True, vmem_limit_bytes=48 * 1024 * 1024
        ),
    )(dqkv, inputs, attn, incoming, qkv_weight, deal)
    return (branch[None], grad_inputs[None], qkv_share, out_share)


def solution(mesh):
    return jax.shard_map(
        body,
        mesh=mesh,
        in_specs=(P("dp", "seq", None), P("dp", "seq", None), P(), P(), P(), P(), P()),
        out_specs=(
            P("dp", "seq", None),
            P("dp", "seq", None),
            P(("seq", "dp"), None),
            P(("seq", "dp"), None),
        ),
        check_vma=False,
    )
```

time: 696 us -> 102 us (0.15)
  waiting for transfers between devices: 428 us -> 0 us
  local copies, waits for them, and re-layouts: 122 us -> 10.7 us
  Pallas kernels: 0 us -> 90.8 us
  blocking collectives: 50.6 us -> 0 us
  matrix products: 39.6 us -> 0 us
  other arithmetic: 30.3 us -> 0 us
  between operations: 15.3 us -> 0.7 us
    unnamed x4 -> x0, waiting for transfers between devices: 404 us -> none
    pallas_call x0 -> x2, Pallas kernels: none -> 90.8 us  [the longest x1 46.7 us: body(): pl.pallas_call(weights, out_shape=[jax.ShapeDtypeStruct((TOK, WIDTH), BF)...]
    broadcast_in_dim x28 -> x0, local copies, waits for them, and re-layouts: 52.5 us -> none  [undilate(): spread = jnp.where(pick[None], values[:, None], jnp.zeros((), values.dtype))]
    all_gather x1 -> x0, blocking collectives: 50.6 us -> none  [body(): lax.all_gather(pack_rows(dilate(key_norm, far_mask), dilate(value, far_ma...]
    dot_general x24 -> x0, matrix products: 39.6 us -> none  [the longest x3 7.15 us: block_forward(): jnp.einsum('qhe,khe->hqk', query_rows, key_rows, preferred_element_type=j...]
    ppermute x6 -> x0, waiting for transfers between devices: 24.1 us -> none  [from_partner(): return lax.ppermute(block, axis, route)]
    another operation x11 -> x0, local copies, waits for them, and re-layouts: 19.5 us -> none  [the longest x7 11.6 us: pack_rows(): jnp.stack([first_rows.reshape(-1, width), second_rows.reshape(-1, width)]...]
    convert_element_type x7 -> x0, local copies, waits for them, and re-layouts: 14.8 us -> none  [the longest x6 13 us: normalize(): wide = rows.astype(jnp.float32)]
  transfers between devices with their start and end apart: 8 -> 0, of which waited for: 6 -> 0; matrix products, arithmetic and copies ran while one was open for 13% -> 0% of each run, Pallas kernels for 0% -> 0%
where the time goes in v1:
time: 102 us
  Pallas kernels  90.8 us (89%)
  local copies, waits for them, and re-layouts  10.7 us (10%)
    pallas_call x1, Pallas kernels, body(): pl.pallas_call(weights, out_shape=[jax.ShapeDtypeStruct((TOK, WIDTH), BF)...  46.7 us
    pallas_call x1, Pallas kernels, body(): pl.pallas_call(attention, out_shape=[jax.ShapeDtypeStruct((TOK, WIDTH), B...  44.1 us
    unnamed x28, local copies, waits for them, and re-layouts  10.7 us

profile of v1, /device:TPU:1, one launch (start us, length us, event | category | flops | bytes accessed | tf_op | source)
XLA Modules:
  0.0 102.2 jit_solution(4987444499016973609)
XLA Ops:
  0.6 0.0 copy-start
  0.6 0.0 copy-start.1
  0.7 1.4 %copy-done.1 = bf16[768,768]{1,0:T(8,128)(2,1)S(1)} copy-done((bf16[768,768]{1,0:T(8,128)(2,1)S(1)}, bf16[768,768]{1,0:T(8,128)(2,1)}, u32[]{:S(2)}) %copy-start.1) | copy-done | bytes 1179672
  2.1 0.0 copy-start.2
  2.1 0.9 copy-done.2
  3.0 0.0 copy-start.4
  3.0 0.9 copy-done.4
  3.9 0.0 copy-start.5
  3.9 1.0 copy-done.5
  4.9 0.0 copy-start.6
  4.9 1.0 copy-done.6
  5.9 0.0 copy-start.7
  5.9 0.9 copy-done.7
  6.8 0.0 copy-start.9
  6.8 0.7 copy-done.9
  7.4 0.0 copy-start.10
  7.4 0.7 copy-done.10
  8.1 0.0 copy-start.11
  8.1 0.7 copy-done.11
  8.8 0.0 copy-start.3
  8.8 0.0 copy-start.8
  8.8 44.1 %shard_map.138 = (bf16[128,768]{1,0:T(8,128)(2,1)S(1)}, bf16[128,768]{1,0:T(8,128)(2,1)S(1)}, bf16[128,2304]{1,0:T(8,128)(2,1)S(1)}) custom-call(f32[12]{0:T(128)S(1)} %copy-done.9, s32[12]{0:T(128)S(1)} %copy-done.10, s32[12]{0:T(128)S(1)} %copy-done.11, bf16[128,768]{1,0:T(8,128)(2,1)S(1)} %bitcast.4, bf16[128,768]{1,0:T(8,128)(2,1)S(1)} %bitcast.6, ...), custom_call_target="tpu_custom_call" | custom-call | tf_op jit(solution)/shard_map/pallas_call | solution.py:527
  52.8 0.0 copy-done
  52.8 0.0 copy-done.3
  52.9 0.0 copy-done.8
  52.9 46.7 %shard_map.139 = (bf16[128,768]{1,0:T(8,128)(2,1)S(1)}, f32[9,768]{1,0:T(8,128)S(1)}, f32[3,768]{1,0:T(4,128)S(1)}) custom-call(bf16[128,2304]{1,0:T(8,128)(2,1)S(1)} %get-tuple-element.11.dqkv_ref, bf16[128,768]{1,0:T(8,128)(2,1)S(1)} %bitcast.5, bf16[128,768]{1,0:T(8,128)(2,1)S(1)} %get-tuple-element.12.attn_ref, bf16[128,768]{1,0:T(8,128)(2,1)S(1)} %bitcast.7, ...), custom_call_target="tpu_custom_call" | custom-call | tf_op jit(solution)/shard_map/pallas_call | solution.py:560
  99.6 0.7 copy.19
  100.3 0.7 copy.20
  100.9 0.6 copy.21
  101.6 0.6 copy.22
Async XLA Ops:
  0.6 52.2 %copy-start = (bf16[2304,768]{1,0:T(8,128)(2,1)S(1)}, bf16[2304,768]{1,0:T(8,128)(2,1)}, u32[]{:S(2)}) copy-start(bf16[2304,768]{1,0:T(8,128)(2,1)} %wqkv_ref.3) | copy-start | bytes 10616836
  0.6 1.4 %copy-start.1 = (bf16[768,768]{1,0:T(8,128)(2,1)S(1)}, bf16[768,768]{1,0:T(8,128)(2,1)}, u32[]{:S(2)}) copy-start(bf16[768,768]{1,0:T(8,128)(2,1)} %wout_ref.1) | copy-start | bytes 3538948
  2.1 0.9 copy-start.2
  3.0 0.9 copy-start.4
  3.9 1.0 copy-start.5
  4.9 1.0 copy-start.6
  5.9 0.9 copy-start.7
  6.8 0.7 copy-start.9
  7.4 0.7 copy-start.10
  8.1 0.7 copy-start.11
  8.8 44.1 %copy-start.3 = (bf16[1,128,768]{2,1,0:T(8,128)(2,1)S(1)}, bf16[1,128,768]{2,1,0:T(8,128)(2,1)}, u32[]{:S(2)}) copy-start(bf16[1,128,768]{2,1,0:T(8,128)(2,1)} %param.11) | copy-start | bytes 589828
  8.8 44.1 %copy-start.8 = (bf16[128,96]{1,0:T(8,128)(2,1)S(1)}, bf16[128,96]{1,0:T(8,128)(2,1)}, u32[]{:S(2)}) copy-start(bf16[128,96]{1,0:T(8,128)(2,1)} %constant.11.clone.deal_ref) | copy-start | bytes 73732

commit v2 on v1

v2 whole, which is shorter than its diff:
```python
import jax
import jax.numpy as jnp
import numpy as np
from jax import lax
from jax.experimental import pallas as pl
from jax.experimental.pallas import tpu as pltpu
from jax.sharding import PartitionSpec as P

BF = jnp.bfloat16
F32 = jnp.float32
MESH = pl.DeviceIdType.MESH
EPS = 1e-06

NY, NZ, NX = 4, 8, 4
TOK = 128
WIDTH = 768
HEADS = 12
HEAD = 64
GROUP = 4
LANES = GROUP * HEAD
GROUPS = HEADS // GROUP
SPAN = 8
NEAR = TOK // SPAN
FAR = 2
PACK = 32
TILES = WIDTH // 128
OWNERS = 2 * NX
QROWS = 3 * WIDTH // NY
OROWS = WIDTH // NY
QOWN, OOWN = QROWS // OWNERS, OROWS // OWNERS
PIECE = QOWN + OOWN
EARLY = 176
LATE = 224


def nn(a, b):
    return lax.dot_general(a, b, (((1,), (0,)), ((), ())), preferred_element_type=F32)


def nt(a, b):
    return lax.dot_general(a, b, (((1,), (1,)), ((), ())), preferred_element_type=F32)


def tn(a, b):
    return lax.dot_general(a, b, (((0,), (0,)), ((), ())), preferred_element_type=F32)


def split(x):
    high = x.astype(BF)
    return high, (x - high.astype(F32)).astype(BF)


def iota(shape, dim):
    return lax.broadcasted_iota(jnp.int32, shape, dim)


def place():
    seq = lax.axis_index("seq")
    return seq, lax.rem(seq, 2), lax.rem(seq // 2, NZ), seq // (2 * NZ)


def at(y, z, core):
    return {"seq": (y * NZ + z) * 2 + core}


def remote(src, dst, send, recv, device):
    return pltpu.make_async_remote_copy(
        src_ref=src, dst_ref=dst, send_sem=send, recv_sem=recv, device_id=device, device_id_type=MESH
    )


def lanes_of(b):
    return slice(b * LANES, (b + 1) * LANES)


def layer(
    scale_ref, near_ref, far_ref, tok_hbm, cot_hbm, wqkv_hbm, wout_hbm,
    block_hbm, compact_hbm, order_hbm, perm_q_hbm, perm_o_hbm, deal_hbm,
    branch_ref, grad_tok_ref, qkv_out, out_out,
    wqkv_ref, wout_ref, block_ref, compact_ref, order_ref, perm_q, perm_o, deal_ref,
    toks, cots, qkv, qn, kn, gr, inv_q, inv_k, p_loc, p_near, p_far, num, den, dq, dk, dv, dqkv, pack,
    near_kv, near_qg, near_s, far_zkv, far_zqg, far_kv, far_qg, far_sz, far_s,
    attn_t, dqkv_t, stage, early_out, early_in, late_out, late_in, q_sum, o_sum, y_send, y_recv, z_send, z_recv,
    loads, sends, r_tok, r_cot, r_ftok, r_fcot, r_nkv, r_nqg, r_ns, r_zkv, r_zqg, r_sz, r_fkv, r_fqg, r_ckv, r_cqg,
    r_fs, r_early, r_late, r_y, r_z,
):
    seq, core, z, y = place()
    x = lax.axis_index("dp")
    mine = lax.rem(seq, SPAN)
    base = seq - mine
    other = 1 - core
    own = core * NX + x

    copies = []
    for n, (src, dst) in enumerate((
        (tok_hbm, toks.at[own]), (wqkv_hbm.at[WIDTH : 3 * WIDTH], wqkv_ref.at[WIDTH : 3 * WIDTH]),
        (block_hbm, block_ref), (cot_hbm, cots.at[own]), (wqkv_hbm.at[:WIDTH], wqkv_ref.at[:WIDTH]),
        (wout_hbm, wout_ref), (order_hbm, order_ref), (compact_hbm, compact_ref), (perm_q_hbm, perm_q),
        (perm_o_hbm, perm_o), (deal_hbm, deal_ref),
    )):
        copy = pltpu.make_async_copy(src, dst, loads.at[n])
        copy.start()
        copies.append(copy)

    z_peers = [lax.rem(z + d, NZ) for d in range(1, NZ)]
    y_peers = [lax.rem(y + d, NY) for d in range(1, NY)]
    x_peers = [lax.rem(x + d, NX) for d in range(1, NX)]
    near_peers = [lax.rem(mine + d, SPAN) for d in range(1, SPAN)]
    near_same = [2 * lax.rem(mine // 2 + d, SPAN // 2) + core for d in range(1, SPAN // 2)]
    near_other = [2 * lax.rem(mine // 2 + d, SPAN // 2) + other for d in range(SPAN // 2)]
    partner = at(y, z, other)
    pair = seq - core

    def owner(o):
        return {"seq": pair + o // NX, "dp": lax.rem(o, NX)}

    owners = [lax.rem(own + d, OWNERS) for d in range(1, OWNERS)]
    barrier = pltpu.get_barrier_semaphore()
    greeted = (
        [at(y, t, core) for t in z_peers]
        + [{"seq": base + t} for t in near_other]
        + [at(t, z, core) for t in y_peers]
        + [at(t, z, other) for t in y_peers]
        + [{"seq": seq, "dp": t} for t in x_peers]
        + [{"seq": pair + other, "dp": t} for t in x_peers]
    )
    for device in greeted:
        pl.semaphore_signal(barrier, inc=1, device_id=device, device_id_type=MESH)
    sent = []

    def send(src, dst, recv, device):
        copy = remote(src, dst, sends.at[len(sent)], recv, device)
        copy.start()
        sent.append(copy)

    def arrived(ref, recv):
        remote(ref, ref, sends.at[0], recv, {"seq": seq}).wait_recv()

    head_lane = iota((1, LANES), 1) // HEAD
    picks_f = [(head_lane == h).astype(F32) for h in range(GROUP)]
    picks = [m.astype(BF) for m in picks_f]

    def spread(x):
        return jnp.concatenate([x * m for m in picks], axis=0)

    def fold(x):
        rows = x.shape[0] // GROUP
        return sum(x[h * rows : (h + 1) * rows] * picks_f[h] for h in range(GROUP))

    wide_head = iota((1, WIDTH), 1) // HEAD
    slim_head = iota((1, 128), 1)
    slim_head = jnp.where(slim_head >= HEADS, slim_head - HEADS, slim_head)
    near_row, far_row = jnp.zeros((1, WIDTH), jnp.int32), jnp.zeros((1, WIDTH), jnp.int32)
    near_slim, far_slim = jnp.zeros((1, 128), jnp.int32), jnp.zeros((1, 128), jnp.int32)
    for h in range(HEADS):
        near_row = jnp.where(wide_head == h, near_ref[h], near_row)
        far_row = jnp.where(wide_head == h, far_ref[h], far_row)
        near_slim = jnp.where(slim_head == h, near_ref[h], near_slim)
        far_slim = jnp.where(slim_head == h, far_ref[h], far_slim)
    near_mask = ((iota((TOK, WIDTH), 0) & (SPAN - 1)) == near_row).astype(F32)
    far_mask = ((iota((TOK, WIDTH), 0) & (TOK // FAR - 1)) == far_row).astype(F32)
    near_bf, far_bf = near_mask.astype(BF), far_mask.astype(BF)
    near_slim = ((iota((TOK, 128), 0) & (SPAN - 1)) == near_slim).astype(F32).astype(BF)
    far_slim = ((iota((TOK, 128), 0) & (TOK // FAR - 1)) == far_slim).astype(F32).astype(BF)
    row, token = iota((NEAR, TOK), 0), iota((NEAR, TOK), 1)
    take_near = (token // SPAN == row).astype(F32).astype(BF)
    take_far = (token // (TOK // FAR) == row).astype(F32).astype(BF)
    take_far_z = ((row // FAR == z) & (token // (TOK // FAR) == (row & 1))).astype(F32).astype(BF)

    def unnear(x, b):
        return jnp.broadcast_to(x[:, None, :], (NEAR, SPAN, LANES)).reshape(TOK, LANES) * near_mask[:, lanes_of(b)]

    def unfar(x, b):
        rows = [jnp.broadcast_to(x[i : i + 1], (TOK // FAR, LANES)) for i in range(FAR)]
        return jnp.concatenate(rows, axis=0) * far_mask[:, lanes_of(b)]

    def norms(columns):
        wide = columns.astype(F32)
        high, low = split(wide * wide)
        inverse = lax.rsqrt(nn(high, block_ref[...]) + nn(low, block_ref[...]) + EPS)
        return inverse, wide * inverse

    far_rows = []

    def leave(pair_of, far_into, near_into):
        pack[2 * FAR * TILES :, :] = jnp.zeros((PACK - 2 * FAR * TILES, 128), F32)
        for i, x_ in enumerate(pair_of):
            picked = nn(take_far, x_ * far_bf)
            far_rows.append(picked.astype(BF))
            for r in range(FAR):
                for t in range(TILES):
                    at_row = (i * FAR + r) * TILES + t
                    pack[at_row : at_row + 1, :] = picked[r : r + 1, 128 * t : 128 * (t + 1)]
        far_into[z] = pack[...].astype(BF)
        for i, x_ in enumerate(pair_of):
            near_into[mine, i] = nn(take_near, x_ * near_bf).astype(BF)

    for n in range(3):
        copies[n].wait()
    tok = toks[own]
    for b in range(GROUPS, 3 * GROUPS):
        qkv[:, lanes_of(b)] = nt(tok, wqkv_ref[lanes_of(b), :]).astype(BF)
    for b in range(GROUPS):
        inverse, unit = norms(qkv[:, lanes_of(GROUPS + b)])
        inv_k[:, lanes_of(b)] = inverse
        kn[:, lanes_of(b)] = unit.astype(BF)
    pl.semaphore_wait(barrier, len(greeted))
    leave((kn[...], qkv[:, 2 * WIDTH :]), far_zkv, near_kv)
    for t in z_peers:
        send(far_zkv.at[z], far_zkv.at[z], r_zkv.at[z], at(y, t, core))
    for t in near_same:
        send(near_kv.at[mine], near_kv.at[mine], r_nkv.at[mine], {"seq": base + t})
    send(near_kv.at[mine], near_kv.at[mine], r_nkv.at[mine], partner)

    for n in range(3, 6):
        copies[n].wait()
    cot = cots[own]
    for b in range(GROUPS):
        qkv[:, lanes_of(b)] = nt(tok, wqkv_ref[lanes_of(b), :]).astype(BF)
        gr[:, lanes_of(b)] = nt(cot, wout_ref[lanes_of(b), :]).astype(BF)
        inverse, unit = norms(qkv[:, lanes_of(b)])
        inv_q[:, lanes_of(b)] = inverse
        qn[:, lanes_of(b)] = unit.astype(BF)
    leave((qn[...], gr[...]), far_zqg, near_qg)
    for t in z_peers:
        send(far_zqg.at[z], far_zqg.at[z], r_zqg.at[z], at(y, t, core))
    for t in near_same:
        send(near_qg.at[mine], near_qg.at[mine], r_nqg.at[mine], {"seq": base + t})
    send(near_qg.at[mine], near_qg.at[mine], r_nqg.at[mine], partner)
    for all_, recv, forward_recv in ((toks, r_tok, r_ftok), (cots, r_cot, r_fcot)):
        for t in x_peers:
            send(all_.at[own], all_.at[own], recv.at[x], {"seq": seq, "dp": t})
        send(all_.at[own], all_.at[own], forward_recv.at[x], partner)

    ones = spread(jnp.ones((TOK, LANES), BF))
    for b in range(GROUPS):
        s = nt(spread(qn[:, lanes_of(b)]), kn[:, lanes_of(b)])
        ps = []
        for h in range(GROUP):
            p = jnp.exp(s[h * TOK : (h + 1) * TOK] * scale_ref[GROUP * b + h])
            p_loc[(GROUP * b + h) * TOK : (GROUP * b + h + 1) * TOK, :] = p
            ps.append(p.astype(BF))
        ps = jnp.concatenate(ps, axis=1)
        num[:, lanes_of(b)] = nn(ps, spread(qkv[:, lanes_of(2 * GROUPS + b)]))
        den[:, lanes_of(b)] = nn(ps, ones)

    for n in range(6, 11):
        copies[n].wait()

    def along_y(packets, recv_z, into, recv):
        for t in z_peers:
            arrived(packets.at[t], recv_z.at[t])
        ordered = nn(order_ref[...], packets[...].reshape(NZ * PACK, 128)).astype(BF)
        for i in range(2):
            for t in range(TILES):
                first = (i * TILES + t) * 16
                into[core, y, i, :, 128 * t : 128 * (t + 1)] = ordered[first : first + 16, :]
        for t in y_peers:
            send(into.at[core, y], into.at[core, y], recv.at[y], at(t, z, core))

    def across(ref, recv):
        for t in near_same:
            arrived(ref.at[t], recv.at[t])
            send(ref.at[t], ref.at[t], recv.at[t], partner)

    def forward(queries, keys, values, p_ref):
        results = []
        for b in range(GROUPS):
            s = nt(spread(queries[:, lanes_of(b)]), keys(b))
            ps = []
            for h in range(GROUP):
                ps.append(jnp.exp(s[h * 16 : (h + 1) * 16] * scale_ref[GROUP * b + h]))
            p = jnp.concatenate(ps, axis=0)
            p_ref[b] = p
            total = jnp.broadcast_to(jnp.sum(p, axis=1, keepdims=True), (GROUP * 16, LANES))
            results.append((fold(nn(p.astype(BF), values(b))), fold(total)))
        return results

    def near_rows(ref, i):
        return lambda b: jnp.concatenate([ref[s, i, :, lanes_of(b)] for s in range(SPAN)], axis=0)

    def far_rows_of(ref, i):
        return lambda b: jnp.concatenate(
            [ref[s, t, i, :, lanes_of(b)] for s in range(2) for t in range(NY)], axis=0
        )

    along_y(far_zkv, r_zkv, far_kv, r_fkv)
    across(near_kv, r_nkv)
    along_y(far_zqg, r_zqg, far_qg, r_fqg)
    for t in near_other:
        arrived(near_kv.at[t], r_nkv.at[t])
    near_q, near_g = near_qg[mine, 0], near_qg[mine, 1]
    for b, (n_part, d_part) in enumerate(forward(near_q, near_rows(near_kv, 0), near_rows(near_kv, 1), p_near)):
        num[:, lanes_of(b)] += unnear(n_part, b)
        den[:, lanes_of(b)] += unnear(d_part, b)
    for t in y_peers:
        arrived(far_kv.at[core, t], r_fkv.at[t])
    send(far_kv.at[core], far_kv.at[core], r_ckv, partner)
    across(near_qg, r_nqg)
    arrived(far_kv.at[other], r_ckv)
    far_k, far_v, far_q, far_g = far_rows
    for b, (n_part, d_part) in enumerate(forward(far_q, far_rows_of(far_kv, 0), far_rows_of(far_kv, 1), p_far)):
        num[:, lanes_of(b)] += unfar(n_part, b)
        den[:, lanes_of(b)] += unfar(d_part, b)

    inverse = 1.0 / den[...]
    attn = (num[...] * inverse).astype(BF)
    high, low = split(inverse)
    slim = nn(high, compact_ref[:, :128]) + nn(low, compact_ref[:, :128])
    high, low = split(gr[...].astype(F32) * attn.astype(F32))
    slim = slim + nn(high, compact_ref[:, 128:]) + nn(low, compact_ref[:, 128:])
    high, low = split(slim)

    def take(selection, mask):
        return nn(selection, high * mask) + nn(selection, low * mask)

    far_sz[z] = take(take_far_z, far_slim)
    for t in z_peers:
        send(far_sz.at[z], far_sz.at[z], r_sz.at[z], at(y, t, core))
    near_slim_rows = take(take_near, near_slim)
    far_slim_rows = take(take_far, far_slim)
    near_s[mine] = near_slim_rows
    for t in near_peers:
        send(near_s.at[mine], near_s.at[mine], r_ns.at[mine], {"seq": base + t})
    for t in y_peers:
        arrived(far_qg.at[core, t], r_fqg.at[t])
    send(far_qg.at[core], far_qg.at[core], r_cqg, partner)

    for b in range(GROUPS):
        g = spread(gr[:, lanes_of(b)])
        grad_p = nt(g, qkv[:, lanes_of(2 * GROUPS + b)])
        ps, ds = [], []
        for h in range(GROUP):
            n = GROUP * b + h
            p = p_loc[n * TOK : (n + 1) * TOK, :] * slim[:, n : n + 1]
            d = scale_ref[n] * p * (grad_p[h * TOK : (h + 1) * TOK] - slim[:, HEADS + n : HEADS + n + 1])
            ps.append(p.astype(BF))
            ds.append(d.astype(BF))
        dq[:, lanes_of(b)] = nn(jnp.concatenate(ds, axis=1), spread(kn[:, lanes_of(b)]))
        dk[:, lanes_of(b)] = tn(jnp.concatenate(ds, axis=0), spread(qn[:, lanes_of(b)]))
        dv[:, lanes_of(b)] = tn(jnp.concatenate(ps, axis=0), g)

    def query_side(grads, keys, values, p_ref, slim_rows, b):
        grad_p = nt(spread(grads[:, lanes_of(b)]), values(b))
        ds = []
        for h in range(GROUP):
            n = GROUP * b + h
            p = p_ref[b, h * 16 : (h + 1) * 16, :] * slim_rows[:, n : n + 1]
            ds.append(
                scale_ref[n] * p * (grad_p[h * 16 : (h + 1) * 16] - slim_rows[:, HEADS + n : HEADS + n + 1])
            )
        return fold(nn(jnp.concatenate(ds, axis=0).astype(BF), keys(b)))

    for b in range(GROUPS):
        near_part = query_side(near_g, near_rows(near_kv, 0), near_rows(near_kv, 1), p_near, near_slim_rows, b)
        far_part = query_side(far_g, far_rows_of(far_kv, 0), far_rows_of(far_kv, 1), p_far, far_slim_rows, b)
        dq[:, lanes_of(b)] += unnear(near_part, b) + unfar(far_part, b)

    def unnormalize(inv_ref, grad, i):
        for b in range(GROUPS):
            inverse = inv_ref[:, lanes_of(b)]
            unit = qkv[:, lanes_of(GROUPS * i + b)].astype(F32) * inverse
            d = grad[:, lanes_of(b)]
            high, low = split(unit * d)
            along = nn(high, block_ref[...]) + nn(low, block_ref[...])
            dqkv[:, lanes_of(GROUPS * i + b)] = (inverse * (d - unit * along)).astype(BF)

    for t in z_peers:
        arrived(far_sz.at[t], r_sz.at[t])
    far_s[core, y] = jnp.sum(far_sz[...], axis=0)
    for t in y_peers:
        send(far_s.at[core, y], far_s.at[core, y], r_fs.at[core, y], at(t, z, core))
        send(far_s.at[core, y], far_s.at[core, y], r_fs.at[core, y], at(t, z, other))
    send(far_s.at[core, y], far_s.at[core, y], r_fs.at[core, y], partner)

    unnormalize(inv_q, dq, 0)
    attn_t[...] = attn.T
    dqkv_t[:WIDTH, :] = dqkv[:, :WIDTH].T
    for t in range(NY):
        dealt = nn(perm_o[...], attn_t[t * OROWS : (t + 1) * OROWS, :])
        for o in range(OWNERS):
            stage[o, t * OOWN : (t + 1) * OOWN, :] = dealt[o * OOWN : (o + 1) * OOWN]

    def deal_rows(t, first):
        dealt = nn(perm_q[...], dqkv_t[t * QROWS : (t + 1) * QROWS, :])
        for o in range(OWNERS):
            stage[o, first : first + QOWN, :] = dealt[o * QOWN : (o + 1) * QOWN]

    deal_rows(0, NY * OOWN)
    for o in range(OWNERS):
        stage[o, EARLY - 8 : EARLY, :] = jnp.zeros((8, 128), F32)
    early_out[...] = stage[:, :EARLY, :].astype(BF)
    for o in owners:
        send(early_out.at[o], early_in.at[own], r_early.at[own], owner(o))
    early_in[own] = early_out[own]
    branch_ref[...] = nn(attn, wout_ref[...]).astype(BF)

    for all_, recv, forward_recv in ((toks, r_tok, r_ftok), (cots, r_cot, r_fcot)):
        for t in x_peers:
            arrived(all_.at[core * NX + t], recv.at[t])
            send(all_.at[core * NX + t], all_.at[core * NX + t], forward_recv.at[t], partner)

    def key_side(keys, values, queries, grads, columns, b):
        q, g = queries(b), grads(b)
        s = nt(spread(keys[:, lanes_of(b)]), q)
        grad_p = nt(spread(values[:, lanes_of(b)]), g)
        ps, ds = [], []
        for h in range(GROUP):
            n = GROUP * b + h
            p = jnp.exp(s[h * 16 : (h + 1) * 16] * scale_ref[n]) * columns[n : n + 1, :]
            ps.append(p)
            ds.append(
                scale_ref[n] * p * (grad_p[h * 16 : (h + 1) * 16] - columns[HEADS + n : HEADS + n + 1, :])
            )
        p, d = jnp.concatenate(ps, axis=0).astype(BF), jnp.concatenate(ds, axis=0).astype(BF)
        return fold(nn(d, q)), fold(nn(p, g))

    for t in near_peers:
        arrived(near_s.at[t], r_ns.at[t])
    for t in near_other:
        arrived(near_qg.at[t], r_nqg.at[t])
    columns = near_s[...].reshape(TOK, 128).T
    near_k, near_v = near_kv[mine, 0], near_kv[mine, 1]
    for b in range(GROUPS):
        k_part, v_part = key_side(near_k, near_v, near_rows(near_qg, 0), near_rows(near_qg, 1), columns, b)
        dk[:, lanes_of(b)] += unnear(k_part, b)
        dv[:, lanes_of(b)] += unnear(v_part, b)

    for o in owners:
        arrived(early_in.at[o], r_early.at[o])
    for t in range(NX):
        arrived(toks.at[other * NX + t], r_ftok.at[t])
        arrived(cots.at[other * NX + t], r_fcot.at[t])

    def factors(ref, rows):
        return jnp.concatenate([ref[o, rows, :] for o in range(OWNERS)], axis=1)

    o_sum[...] = nn(factors(early_in, slice(0, NY * OOWN)), cots[...].reshape(OWNERS * TOK, WIDTH))
    tokens = toks[...].reshape(OWNERS * TOK, WIDTH)
    q_sum[: EARLY - NY * OOWN, :] = nn(factors(early_in, slice(NY * OOWN, EARLY)), tokens)

    arrived(far_qg.at[other], r_cqg)
    for t in y_peers:
        arrived(far_s.at[core, t], r_fs.at[core, t])
    for t in range(NY):
        arrived(far_s.at[other, t], r_fs.at[other, t])
    columns = far_s[...].reshape(TOK, 128).T
    for b in range(GROUPS):
        k_part, v_part = key_side(far_k, far_v, far_rows_of(far_qg, 0), far_rows_of(far_qg, 1), columns, b)
        dk[:, lanes_of(b)] += unfar(k_part, b)
        dv[:, lanes_of(b)] += unfar(v_part, b)

    unnormalize(inv_k, dk, 1)
    dqkv[:, 2 * WIDTH :] = dv[...].astype(BF)
    dqkv_t[WIDTH:, :] = dqkv[:, WIDTH:].T
    for t in range(1, NY):
        deal_rows(t, (t - 1) * QOWN)
    for o in range(OWNERS):
        stage[o, LATE - 8 : LATE, :] = jnp.zeros((8, 128), F32)
    late_out[...] = stage[...].astype(BF)
    for o in owners:
        send(late_out.at[o], late_in.at[own], r_late.at[own], owner(o))
    late_in[own] = late_out[own]
    grad_tok_ref[...] = nn(dqkv[...], wqkv_ref[...]).astype(BF)
    for o in owners:
        arrived(late_in.at[o], r_late.at[o])
    late = nn(factors(late_in, slice(0, LATE)), tokens)
    q_sum[QOWN:, :] = late[: (NY - 1) * QOWN]

    y_right, y_left = at(lax.rem(y + 1, NY), z, core), at(lax.rem(y + NY - 1, NY), z, core)
    a, b_ = slice(0, PIECE // 2), slice(PIECE // 2, PIECE)

    def piece(t):
        q_rows = pl.ds(pl.multiple_of(t * QOWN, 8), QOWN)
        o_rows = pl.ds(pl.multiple_of(t * OOWN, 8), OOWN)
        return jnp.concatenate([q_sum[q_rows, :], o_sum[o_rows, :]], axis=0)

    def y_out(slot, part, device):
        y_send[slot] = part.astype(BF)
        send(y_send.at[slot], y_recv.at[slot], r_y.at[slot], device)

    def y_in(slot):
        arrived(y_recv.at[slot], r_y.at[slot])
        return y_recv[slot].astype(F32)

    part = piece(lax.rem(y + 2, NY))
    y_out(0, part[a], y_right)
    y_out(1, part[b_], y_left)
    right_part, left_part = piece(lax.rem(y + 1, NY)), piece(lax.rem(y + NY - 1, NY))
    y_out(2, right_part[b_], y_right)
    y_out(4, left_part[a], y_left)
    y_out(3, right_part[a] + y_in(0), y_right)
    y_out(5, left_part[b_] + y_in(1), y_left)
    part = piece(y)
    part = jnp.concatenate([part[a] + y_in(4) + y_in(3), part[b_] + y_in(2) + y_in(5)], axis=0)

    dealt = nn(deal_ref[...], part.astype(BF)).astype(BF)
    for t in range(NZ):
        z_send[t] = dealt[16 * t : 16 * (t + 1), :]
    for t in z_peers:
        send(z_send.at[t], z_recv.at[z], r_z.at[z], at(y, t, core))
    z_recv[z] = z_send[z]
    for t in z_peers:
        arrived(z_recv.at[t], r_z.at[t])
    share = jnp.sum(z_recv[...].astype(F32), axis=0)
    qkv_out[...] = share[: QOWN // NZ]
    out_out[...] = share[QOWN // NZ : PIECE // NZ]
    for copy in sent:
        copy.wait_send()


def constants():
    lane = np.arange(WIDTH)
    block = (lane[:LANES, None] // HEAD == lane[None, :LANES] // HEAD).astype(np.float32)
    compact = np.zeros((WIDTH, 256), np.float32)
    compact[np.arange(HEADS) * HEAD, np.arange(HEADS)] = 1
    compact[lane, 128 + HEADS + lane // HEAD] = 1
    order = np.zeros((2 * TILES * 16, NZ * PACK), np.float32)
    for t in range(2):
        for j in range(TILES):
            for s in range(NZ):
                for i in range(FAR):
                    order[(t * TILES + j) * 16 + s * FAR + i, s * PACK + (t * FAR + i) * TILES + j] = 1

    def deal_out(each):
        index = np.arange(NZ * OWNERS * each).reshape(NZ, OWNERS, each).transpose(1, 0, 2).reshape(-1)
        return np.eye(index.size, dtype=np.float32)[index]

    deal = np.zeros((NZ * 16, PIECE), np.float32)
    for t in range(NZ):
        for i in range(9):
            deal[t * 16 + i, t * 9 + i] = 1
        for i in range(3):
            deal[t * 16 + 9 + i, QOWN + t * 3 + i] = 1
    return [jnp.asarray(m, BF) for m in (block, compact, order, deal_out(9), deal_out(3), deal)]


def body(tokens, cotangent, qkv_weight, out_weight, logit_scale, near_offsets, far_offsets):
    fixed = constants()
    smem = pl.BlockSpec(memory_space=pltpu.SMEM)
    hbm = pl.BlockSpec(memory_space=pltpu.HBM)
    vmem = pl.BlockSpec(memory_space=pltpu.VMEM)
    dma = pltpu.SemaphoreType.DMA
    wide_bf = pltpu.VMEM((TOK, WIDTH), BF)
    wide = pltpu.VMEM((TOK, WIDTH), F32)

    def held(*shape):
        return pltpu.VMEM(shape, BF)

    def held_f32(*shape):
        return pltpu.VMEM(shape, F32)

    branch, grad_inputs, qkv_share, out_share = pl.pallas_call(
        layer,
        out_shape=[
            jax.ShapeDtypeStruct((TOK, WIDTH), BF),
            jax.ShapeDtypeStruct((TOK, WIDTH), BF),
            jax.ShapeDtypeStruct((9, WIDTH), F32),
            jax.ShapeDtypeStruct((3, WIDTH), F32),
        ],
        in_specs=[smem] * 3 + [hbm] * 10,
        out_specs=[vmem] * 4,
        scratch_shapes=[
            held(3 * WIDTH, WIDTH), held(WIDTH, WIDTH), *[held(*m.shape) for m in fixed],
            held(OWNERS, TOK, WIDTH), held(OWNERS, TOK, WIDTH),
            held(TOK, 3 * WIDTH), wide_bf, wide_bf, wide_bf, wide, wide,
            held_f32(HEADS * TOK, 128), held_f32(GROUPS, GROUP * 16, 128), held_f32(GROUPS, GROUP * 16, 128),
            wide, wide, wide, wide, wide, held(TOK, 3 * WIDTH), held_f32(PACK, 128),
            held(SPAN, 2, NEAR, WIDTH), held(SPAN, 2, NEAR, WIDTH), held_f32(SPAN, NEAR, 128),
            held(NZ, PACK, 128), held(NZ, PACK, 128),
            held(2, NY, 2, 16, WIDTH), held(2, NY, 2, 16, WIDTH), held_f32(NZ, 16, 128), held_f32(2, NY, 16, 128),
            held(WIDTH, TOK), held(3 * WIDTH, TOK), held_f32(OWNERS, LATE, 128),
            held(OWNERS, EARLY, 128), held(OWNERS, EARLY, 128), held(OWNERS, LATE, 128), held(OWNERS, LATE, 128),
            held_f32(NY * QOWN, WIDTH), held_f32(NY * OOWN, WIDTH),
            held(6, PIECE // 2, WIDTH), held(6, PIECE // 2, WIDTH),
            held(NZ, 16, WIDTH), held(NZ, 16, WIDTH),
            dma((11,)), dma((112,)),
            dma((4,)), dma((4,)), dma((4,)), dma((4,)),
            dma((8,)), dma((8,)), dma((8,)), dma((8,)), dma((8,)), dma((8,)), dma((4,)), dma((4,)), dma, dma,
            dma((2, 4)), dma((8,)), dma((8,)), dma((6,)), dma((8,)),
        ],
        compiler_params=pltpu.CompilerParams(
            collective_id=0, has_side_effects=True, vmem_limit_bytes=56 * 1024 * 1024
        ),
    )(logit_scale, near_offsets, far_offsets, tokens[0], cotangent[0], qkv_weight, out_weight, *fixed)
    return (branch[None], grad_inputs[None], qkv_share, out_share)


def solution(mesh):
    return jax.shard_map(
        body,
        mesh=mesh,
        in_specs=(P("dp", "seq", None), P("dp", "seq", None), P(), P(), P(), P(), P()),
        out_specs=(
            P("dp", "seq", None),
            P("dp", "seq", None),
            P(("seq", "dp"), None),
            P(("seq", "dp"), None),
        ),
        check_vma=False,
    )
```

time: 102 us -> 72 us (0.71); the launches traced: 102 us -> 71.1 us
  Pallas kernels: 90.8 us -> 64.5 us
  local copies, waits for them, and re-layouts: 10.7 us -> 5.96 us
    pallas_call x2 -> x1, Pallas kernels: 90.8 us -> 64.5 us  [body(): pl.pallas_call(layer, out_shape=[jax.ShapeDtypeStruct((TOK, WIDTH), BF),...]
    unnamed x28 -> x4, local copies, waits for them, and re-layouts: 10.7 us -> 5.96 us
where the time goes in v2:
time: 72 us; the launch traced here: 71.1 us
  Pallas kernels  64.5 us (90%)
  local copies, waits for them, and re-layouts  5.96 us (8%)
    pallas_call x1, Pallas kernels, body(): pl.pallas_call(layer, out_shape=[jax.ShapeDtypeStruct((TOK, WIDTH), BF),...  64.5 us
    unnamed x4, local copies, waits for them, and re-layouts  5.96 us

profile of v2, /device:TPU:1, one launch (start us, length us, event | category | flops | bytes accessed | tf_op | source)
XLA Modules:
  0.0 71.1 jit_solution(9946972015555406113)
XLA Ops:
  0.6 64.5 %shard_map.156 = (bf16[128,768]{1,0:T(8,128)(2,1)}, bf16[128,768]{1,0:T(8,128)(2,1)}, f32[9,768]{1,0:T(8,128)}, f32[3,768]{1,0:T(4,128)}) custom-call(f32[12]{0:T(128)} %scale_ref.1, s32[12]{0:T(128)} %near_ref.1, s32[12]{0:T(128)} %far_ref.1, bf16[128,768]{1,0:T(8,128)(2,1)} %bitcast.4, bf16[128,768]{1,0:T(8,128)(2,1)} %bitcast.5, ...), custom_call_target="tpu_custom_call" | custom-call | tf_op jit(solution)/shard_map/pallas_call | solution.py:553
  65.2 1.6 %copy.21 = bf16[1,128,768]{2,1,0:T(8,128)(2,1)} copy(bf16[1,128,768]{2,1,0:T(8,128)(2,1)} %bitcast.7) | data formatting | bytes 393216
  66.8 1.6 %copy.22 = bf16[1,128,768]{2,1,0:T(8,128)(2,1)} copy(bf16[1,128,768]{2,1,0:T(8,128)(2,1)} %bitcast.6) | data formatting | bytes 393216
  68.4 1.4 %copy.23 = f32[9,768]{1,0:T(8,128)} copy(f32[9,768]{1,0:T(8,128)} %get-tuple-element.18) | data formatting | bytes 55296
  69.8 1.3 %copy.24 = f32[3,768]{1,0:T(4,128)} copy(f32[3,768]{1,0:T(4,128)} %get-tuple-element.19) | data formatting | bytes 18432

commit v3 on v2

--- a/solution.py
+++ b/solution.py
@@ -91,16 +91,23 @@
     other = 1 - core
     own = core * NX + x
 
-    copies = []
-    for n, (src, dst) in enumerate((
-        (tok_hbm, toks.at[own]), (wqkv_hbm.at[WIDTH : 3 * WIDTH], wqkv_ref.at[WIDTH : 3 * WIDTH]),
-        (block_hbm, block_ref), (cot_hbm, cots.at[own]), (wqkv_hbm.at[:WIDTH], wqkv_ref.at[:WIDTH]),
-        (wout_hbm, wout_ref), (order_hbm, order_ref), (compact_hbm, compact_ref), (perm_q_hbm, perm_q),
-        (perm_o_hbm, perm_o), (deal_hbm, deal_ref),
-    )):
-        copy = pltpu.make_async_copy(src, dst, loads.at[n])
+    loading = []
+
+    def load(src, dst):
+        copy = pltpu.make_async_copy(src, dst, loads.at[len(loading)])
         copy.start()
-        copies.append(copy)
+        loading.append(copy)
+
+    def load_rows(src, dst, start, stop):
+        for first in range(start, stop, LANES):
+            load(src.at[first : first + LANES], dst.at[first : first + LANES])
+
+    load(tok_hbm, toks.at[own])
+    load(block_hbm, block_ref)
+    load_rows(wqkv_hbm, wqkv_ref, WIDTH, 3 * WIDTH)
+    load(cot_hbm, cots.at[own])
+    load_rows(wqkv_hbm, wqkv_ref, 0, WIDTH)
+    load_rows(wout_hbm, wout_ref, 0, WIDTH)
 
     z_peers = [lax.rem(z + d, NZ) for d in range(1, NZ)]
     y_peers = [lax.rem(y + d, NY) for d in range(1, NY)]
@@ -195,10 +202,11 @@
         for i, x_ in enumerate(pair_of):
             near_into[mine, i] = nn(take_near, x_ * near_bf).astype(BF)
 
-    for n in range(3):
-        copies[n].wait()
+    for copy in loading[:2]:
+        copy.wait()
     tok = toks[own]
     for b in range(GROUPS, 3 * GROUPS):
+        loading[2 + b - GROUPS].wait()
         qkv[:, lanes_of(b)] = nt(tok, wqkv_ref[lanes_of(b), :]).astype(BF)
     for b in range(GROUPS):
         inverse, unit = norms(qkv[:, lanes_of(GROUPS + b)])
@@ -212,8 +220,14 @@
         send(near_kv.at[mine], near_kv.at[mine], r_nkv.at[mine], {"seq": base + t})
     send(near_kv.at[mine], near_kv.at[mine], r_nkv.at[mine], partner)
 
-    for n in range(3, 6):
-        copies[n].wait()
+    first = len(loading)
+    load(order_hbm, order_ref)
+    load(compact_hbm, compact_ref)
+    load(perm_q_hbm, perm_q)
+    load(perm_o_hbm, perm_o)
+    load(deal_hbm, deal_ref)
+    for copy in loading[2 + 2 * GROUPS : first]:
+        copy.wait()
     cot = cots[own]
     for b in range(GROUPS):
         qkv[:, lanes_of(b)] = nt(tok, wqkv_ref[lanes_of(b), :]).astype(BF)
@@ -222,11 +236,6 @@
         inv_q[:, lanes_of(b)] = inverse
         qn[:, lanes_of(b)] = unit.astype(BF)
     leave((qn[...], gr[...]), far_zqg, near_qg)
-    for t in z_peers:
-        send(far_zqg.at[z], far_zqg.at[z], r_zqg.at[z], at(y, t, core))
-    for t in near_same:
-        send(near_qg.at[mine], near_qg.at[mine], r_nqg.at[mine], {"seq": base + t})
-    send(near_qg.at[mine], near_qg.at[mine], r_nqg.at[mine], partner)
     for all_, recv, forward_recv in ((toks, r_tok, r_ftok), (cots, r_cot, r_fcot)):
         for t in x_peers:
             send(all_.at[own], all_.at[own], recv.at[x], {"seq": seq, "dp": t})
@@ -244,8 +253,8 @@
         num[:, lanes_of(b)] = nn(ps, spread(qkv[:, lanes_of(2 * GROUPS + b)]))
         den[:, lanes_of(b)] = nn(ps, ones)
 
-    for n in range(6, 11):
-        copies[n].wait()
+    for copy in loading[first:]:
+        copy.wait()
 
     def along_y(packets, recv_z, into, recv):
         for t in z_peers:
@@ -286,7 +295,11 @@
 
     along_y(far_zkv, r_zkv, far_kv, r_fkv)
     across(near_kv, r_nkv)
-    along_y(far_zqg, r_zqg, far_qg, r_fqg)
+    for t in z_peers:
+        send(far_zqg.at[z], far_zqg.at[z], r_zqg.at[z], at(y, t, core))
+    for t in near_same:
+        send(near_qg.at[mine], near_qg.at[mine], r_nqg.at[mine], {"seq": base + t})
+    send(near_qg.at[mine], near_qg.at[mine], r_nqg.at[mine], partner)
     for t in near_other:
         arrived(near_kv.at[t], r_nkv.at[t])
     near_q, near_g = near_qg[mine, 0], near_qg[mine, 1]
@@ -296,7 +309,7 @@
     for t in y_peers:
         arrived(far_kv.at[core, t], r_fkv.at[t])
     send(far_kv.at[core], far_kv.at[core], r_ckv, partner)
-    across(near_qg, r_nqg)
+    along_y(far_zqg, r_zqg, far_qg, r_fqg)
     arrived(far_kv.at[other], r_ckv)
     far_k, far_v, far_q, far_g = far_rows
     for b, (n_part, d_part) in enumerate(forward(far_q, far_rows_of(far_kv, 0), far_rows_of(far_kv, 1), p_far)):
@@ -322,9 +335,7 @@
     near_s[mine] = near_slim_rows
     for t in near_peers:
         send(near_s.at[mine], near_s.at[mine], r_ns.at[mine], {"seq": base + t})
-    for t in y_peers:
-        arrived(far_qg.at[core, t], r_fqg.at[t])
-    send(far_qg.at[core], far_qg.at[core], r_cqg, partner)
+    across(near_qg, r_nqg)
 
     for b in range(GROUPS):
         g = spread(gr[:, lanes_of(b)])
@@ -364,6 +375,10 @@
             high, low = split(unit * d)
             along = nn(high, block_ref[...]) + nn(low, block_ref[...])
             dqkv[:, lanes_of(GROUPS * i + b)] = (inverse * (d - unit * along)).astype(BF)
+
+    for t in y_peers:
+        arrived(far_qg.at[core, t], r_fqg.at[t])
+    send(far_qg.at[core], far_qg.at[core], r_cqg, partner)
 
     for t in z_peers:
         arrived(far_sz.at[t], r_sz.at[t])
@@ -426,19 +441,6 @@
         dk[:, lanes_of(b)] += unnear(k_part, b)
         dv[:, lanes_of(b)] += unnear(v_part, b)
 
-    for o in owners:
-        arrived(early_in.at[o], r_early.at[o])
-    for t in range(NX):
-        arrived(toks.at[other * NX + t], r_ftok.at[t])
-        arrived(cots.at[other * NX + t], r_fcot.at[t])
-
-    def factors(ref, rows):
-        return jnp.concatenate([ref[o, rows, :] for o in range(OWNERS)], axis=1)
-
-    o_sum[...] = nn(factors(early_in, slice(0, NY * OOWN)), cots[...].reshape(OWNERS * TOK, WIDTH))
-    tokens = toks[...].reshape(OWNERS * TOK, WIDTH)
-    q_sum[: EARLY - NY * OOWN, :] = nn(factors(early_in, slice(NY * OOWN, EARLY)), tokens)
-
     arrived(far_qg.at[other], r_cqg)
     for t in y_peers:
         arrived(far_s.at[core, t], r_fs.at[core, t])
@@ -461,6 +463,18 @@
     for o in owners:
         send(late_out.at[o], late_in.at[own], r_late.at[own], owner(o))
     late_in[own] = late_out[own]
+    for o in owners:
+        arrived(early_in.at[o], r_early.at[o])
+    for t in range(NX):
+        arrived(toks.at[other * NX + t], r_ftok.at[t])
+        arrived(cots.at[other * NX + t], r_fcot.at[t])
+
+    def factors(ref, rows):
+        return jnp.concatenate([ref[o, rows, :] for o in range(OWNERS)], axis=1)
+
+    o_sum[...] = nn(factors(early_in, slice(0, NY * OOWN)), cots[...].reshape(OWNERS * TOK, WIDTH))
+    tokens = toks[...].reshape(OWNERS * TOK, WIDTH)
+    q_sum[: EARLY - NY * OOWN, :] = nn(factors(early_in, slice(NY * OOWN, EARLY)), tokens)
     grad_tok_ref[...] = nn(dqkv[...], wqkv_ref[...]).astype(BF)
     for o in owners:
         arrived(late_in.at[o], r_late.at[o])
@@ -509,6 +523,15 @@
         copy.wait_send()
 
 
+def finish(*refs):
+    count = len(refs) // 2
+    copies = [pltpu.make_async_copy(refs[n], refs[count + n], refs[-1].at[n]) for n in range(count)]
+    for copy in copies:
+        copy.start()
+    for copy in copies:
+        copy.wait()
+
+
 def constants():
     lane = np.arange(WIDTH)
     block = (lane[:LANES, None] // HEAD == lane[None, :LANES] // HEAD).astype(np.float32)
@@ -550,14 +573,15 @@
     def held_f32(*shape):
         return pltpu.VMEM(shape, F32)
 
-    branch, grad_inputs, qkv_share, out_share = pl.pallas_call(
+    results = [
+        jax.ShapeDtypeStruct((TOK, WIDTH), BF),
+        jax.ShapeDtypeStruct((TOK, WIDTH), BF),
+        jax.ShapeDtypeStruct((9, WIDTH), F32),
+        jax.ShapeDtypeStruct((3, WIDTH), F32),
+    ]
+    values = pl.pallas_call(
         layer,
-        out_shape=[
-            jax.ShapeDtypeStruct((TOK, WIDTH), BF),
-            jax.ShapeDtypeStruct((TOK, WIDTH), BF),
-            jax.ShapeDtypeStruct((9, WIDTH), F32),
-            jax.ShapeDtypeStruct((3, WIDTH), F32),
-        ],
+        out_shape=results,
         in_specs=[smem] * 3 + [hbm] * 10,
         out_specs=[vmem] * 4,
         scratch_shapes=[
@@ -574,7 +598,7 @@
             held_f32(NY * QOWN, WIDTH), held_f32(NY * OOWN, WIDTH),
             held(6, PIECE // 2, WIDTH), held(6, PIECE // 2, WIDTH),
             held(NZ, 16, WIDTH), held(NZ, 16, WIDTH),
-            dma((11,)), dma((112,)),
+            dma((24,)), dma((112,)),
             dma((4,)), dma((4,)), dma((4,)), dma((4,)),
             dma((8,)), dma((8,)), dma((8,)), dma((8,)), dma((8,)), dma((8,)), dma((4,)), dma((4,)), dma, dma,
             dma((2, 4)), dma((8,)), dma((8,)), dma((6,)), dma((8,)),
@@ -583,6 +607,14 @@
             collective_id=0, has_side_effects=True, vmem_limit_bytes=56 * 1024 * 1024
         ),
     )(logit_scale, near_offsets, far_offsets, tokens[0], cotangent[0], qkv_weight, out_weight, *fixed)
+    branch, grad_inputs, qkv_share, out_share = pl.pallas_call(
+        finish,
+        out_shape=results,
+        in_specs=[pl.BlockSpec(memory_space=pl.ANY)] * 4,
+        out_specs=[pl.BlockSpec(memory_space=pl.ANY)] * 4,
+        scratch_shapes=[dma((4,))],
+        compiler_params=pltpu.CompilerParams(vmem_limit_bytes=1024 * 1024),
+    )(*values)
     return (branch[None], grad_inputs[None], qkv_share, out_share)
 
 

time: 72 us -> 64.9 us (0.901)
  the two profiles are of different devices: /device:TPU:1 before, /device:TPU:16 now
where the time goes in v3:
time: 64.9 us; the launch traced here: 64.6 us
  Pallas kernels  60.6 us (93%)
  local copies, waits for them, and re-layouts  3.35 us (5%)
  between operations  0.65 us (1%)
    pallas_call x1, Pallas kernels, body(): pl.pallas_call(layer, out_shape=results, in_specs=[smem] * 3 + [hbm] * 10...  59.8 us
    unnamed x8, local copies, waits for them, and re-layouts  3.35 us

profile of v3, /device:TPU:16, one launch (start us, length us, event | category | flops | bytes accessed | tf_op | source)
XLA Modules:
  0.0 64.6 jit_solution(10306246885554019561)
XLA Ops:
  0.6 59.8 %shard_map.156 = (bf16[128,768]{1,0:T(8,128)(2,1)}, bf16[128,768]{1,0:T(8,128)(2,1)}, f32[9,768]{1,0:T(8,128)}, f32[3,768]{1,0:T(4,128)}) custom-call(f32[12]{0:T(128)} %scale_ref.1, s32[12]{0:T(128)} %near_ref.1, s32[12]{0:T(128)} %far_ref.1, bf16[128,768]{1,0:T(8,128)(2,1)} %bitcast.4, bf16[128,768]{1,0:T(8,128)(2,1)} %bitcast.5, ...), custom_call_target="tpu_custom_call" | custom-call | tf_op jit(solution)/shard_map/pallas_call | solution.py:582
  60.5 0.0 copy-start
  60.5 0.9 %copy-done = bf16[128,768]{1,0:T(8,128)(2,1)S(1)} copy-done((bf16[128,768]{1,0:T(8,128)(2,1)S(1)}, bf16[128,768]{1,0:T(8,128)(2,1)}, u32[]{:S(2)}) %copy-start) | copy-done | bytes 196632
  61.4 0.0 copy-start.1
  61.4 0.9 %copy-done.1 = bf16[128,768]{1,0:T(8,128)(2,1)S(1)} copy-done((bf16[128,768]{1,0:T(8,128)(2,1)S(1)}, bf16[128,768]{1,0:T(8,128)(2,1)}, u32[]{:S(2)}) %copy-start.1) | copy-done | bytes 196632
  62.3 0.0 copy-start.2
  62.3 0.8 %copy-done.2 = f32[9,768]{1,0:T(8,128)S(1)} copy-done((f32[9,768]{1,0:T(8,128)S(1)}, f32[9,768]{1,0:T(8,128)}, u32[]{:S(2)}) %copy-start.2) | copy-done | bytes 27672
  63.1 0.0 copy-start.3
  63.1 0.7 %copy-done.3 = f32[3,768]{1,0:T(4,128)S(1)} copy-done((f32[3,768]{1,0:T(4,128)S(1)}, f32[3,768]{1,0:T(4,128)}, u32[]{:S(2)}) %copy-start.3) | copy-done | bytes 9240
  63.9 0.8 %shard_map.157 = (bf16[128,768]{1,0:T(8,128)(2,1)}, bf16[128,768]{1,0:T(8,128)(2,1)}, f32[9,768]{1,0:T(8,128)}, f32[3,768]{1,0:T(4,128)}) custom-call(bf16[128,768]{1,0:T(8,128)(2,1)S(1)} %copy-done, bf16[128,768]{1,0:T(8,128)(2,1)S(1)} %copy-done.1, f32[9,768]{1,0:T(8,128)S(1)} %copy-done.2, f32[3,768]{1,0:T(4,128)S(1)} %copy-done.3), custom_call_target="tpu_custom_call" | custom-call | tf_op jit(solution)/shard_map/pallas_call | solution.py:610
Async XLA Ops:
  60.5 0.9 %copy-start = (bf16[128,768]{1,0:T(8,128)(2,1)S(1)}, bf16[128,768]{1,0:T(8,128)(2,1)}, u32[]{:S(2)}) copy-start(bf16[128,768]{1,0:T(8,128)(2,1)} %get-tuple-element.12.refs_0_) | copy-start | bytes 589828
  61.4 0.9 %copy-start.1 = (bf16[128,768]{1,0:T(8,128)(2,1)S(1)}, bf16[128,768]{1,0:T(8,128)(2,1)}, u32[]{:S(2)}) copy-start(bf16[128,768]{1,0:T(8,128)(2,1)} %get-tuple-element.13.refs_1_) | copy-start | bytes 589828
  62.3 0.8 %copy-start.2 = (f32[9,768]{1,0:T(8,128)S(1)}, f32[9,768]{1,0:T(8,128)}, u32[]{:S(2)}) copy-start(f32[9,768]{1,0:T(8,128)} %get-tuple-element.14.refs_2_) | copy-start | bytes 82948
  63.1 0.7 %copy-start.3 = (f32[3,768]{1,0:T(4,128)S(1)}, f32[3,768]{1,0:T(4,128)}, u32[]{:S(2)}) copy-start(f32[3,768]{1,0:T(4,128)} %get-tuple-element.15.refs_3_) | copy-start | bytes 27652

commit v4 on v3

--- a/solution.py
+++ b/solution.py
@@ -80,9 +80,9 @@
     wqkv_ref, wout_ref, block_ref, compact_ref, order_ref, perm_q, perm_o, deal_ref,
     toks, cots, qkv, qn, kn, gr, inv_q, inv_k, p_loc, p_near, p_far, num, den, dq, dk, dv, dqkv, pack,
     near_kv, near_qg, near_s, far_zkv, far_zqg, far_kv, far_qg, far_sz, far_s,
-    attn_t, dqkv_t, stage, early_out, early_in, late_out, late_in, q_sum, o_sum, y_send, y_recv, z_send, z_recv,
+    attn_t, dqkv_t, stage, corr, chosen, early_out, early_in, late_out, late_in, q_sum, o_sum, y_send, y_recv, z_send, z_recv,
     loads, sends, r_tok, r_cot, r_ftok, r_fcot, r_nkv, r_nqg, r_ns, r_zkv, r_zqg, r_sz, r_fkv, r_fqg, r_ckv, r_cqg,
-    r_fs, r_early, r_late, r_y, r_z,
+    r_fs, r_early, r_late, r_corr, r_y, r_z,
 ):
     seq, core, z, y = place()
     x = lax.axis_index("dp")
@@ -189,16 +189,19 @@
 
     far_rows = []
 
-    def leave(pair_of, far_into, near_into):
+    def packed(pair_of):
         pack[2 * FAR * TILES :, :] = jnp.zeros((PACK - 2 * FAR * TILES, 128), F32)
-        for i, x_ in enumerate(pair_of):
-            picked = nn(take_far, x_ * far_bf)
-            far_rows.append(picked.astype(BF))
+        for i, picked in enumerate(pair_of):
             for r in range(FAR):
                 for t in range(TILES):
                     at_row = (i * FAR + r) * TILES + t
                     pack[at_row : at_row + 1, :] = picked[r : r + 1, 128 * t : 128 * (t + 1)]
-        far_into[z] = pack[...].astype(BF)
+        return pack[...].astype(BF)
+
+    def leave(pair_of, far_into, near_into):
+        picked = [nn(take_far, x_ * far_bf) for x_ in pair_of]
+        far_rows.extend(x_.astype(BF) for x_ in picked)
+        far_into[z] = packed(picked)
         for i, x_ in enumerate(pair_of):
             near_into[mine, i] = nn(take_near, x_ * near_bf).astype(BF)
 
@@ -216,9 +219,6 @@
     leave((kn[...], qkv[:, 2 * WIDTH :]), far_zkv, near_kv)
     for t in z_peers:
         send(far_zkv.at[z], far_zkv.at[z], r_zkv.at[z], at(y, t, core))
-    for t in near_same:
-        send(near_kv.at[mine], near_kv.at[mine], r_nkv.at[mine], {"seq": base + t})
-    send(near_kv.at[mine], near_kv.at[mine], r_nkv.at[mine], partner)
 
     first = len(loading)
     load(order_hbm, order_ref)
@@ -236,6 +236,9 @@
         inv_q[:, lanes_of(b)] = inverse
         qn[:, lanes_of(b)] = unit.astype(BF)
     leave((qn[...], gr[...]), far_zqg, near_qg)
+    for t in near_same:
+        send(near_kv.at[mine], near_kv.at[mine], r_nkv.at[mine], {"seq": base + t})
+    send(near_kv.at[mine], near_kv.at[mine], r_nkv.at[mine], partner)
     for all_, recv, forward_recv in ((toks, r_tok, r_ftok), (cots, r_cot, r_fcot)):
         for t in x_peers:
             send(all_.at[own], all_.at[own], recv.at[x], {"seq": seq, "dp": t})
@@ -271,6 +274,12 @@
         for t in near_same:
             arrived(ref.at[t], recv.at[t])
             send(ref.at[t], ref.at[t], recv.at[t], partner)
+
+    def hand_over(ref, recv, recv_core):
+        send(ref.at[core, y], ref.at[core, y], recv_core.at[y], partner)
+        for t in y_peers:
+            arrived(ref.at[core, t], recv.at[t])
+            send(ref.at[core, t], ref.at[core, t], recv_core.at[t], partner)
 
     def forward(queries, keys, values, p_ref):
         results = []
@@ -306,11 +315,10 @@
     for b, (n_part, d_part) in enumerate(forward(near_q, near_rows(near_kv, 0), near_rows(near_kv, 1), p_near)):
         num[:, lanes_of(b)] += unnear(n_part, b)
         den[:, lanes_of(b)] += unnear(d_part, b)
-    for t in y_peers:
-        arrived(far_kv.at[core, t], r_fkv.at[t])
-    send(far_kv.at[core], far_kv.at[core], r_ckv, partner)
+    hand_over(far_kv, r_fkv, r_ckv)
     along_y(far_zqg, r_zqg, far_qg, r_fqg)
-    arrived(far_kv.at[other], r_ckv)
+    for t in range(NY):
+        arrived(far_kv.at[other, t], r_ckv.at[t])
     far_k, far_v, far_q, far_g = far_rows
     for b, (n_part, d_part) in enumerate(forward(far_q, far_rows_of(far_kv, 0), far_rows_of(far_kv, 1), p_far)):
         num[:, lanes_of(b)] += unfar(n_part, b)
@@ -367,18 +375,18 @@
         far_part = query_side(far_g, far_rows_of(far_kv, 0), far_rows_of(far_kv, 1), p_far, far_slim_rows, b)
         dq[:, lanes_of(b)] += unnear(near_part, b) + unfar(far_part, b)
 
+    def through(inverse, unit, d):
+        high, low = split(unit * d)
+        along = nn(high, block_ref[...]) + nn(low, block_ref[...])
+        return inverse * (d - unit * along)
+
     def unnormalize(inv_ref, grad, i):
         for b in range(GROUPS):
             inverse = inv_ref[:, lanes_of(b)]
             unit = qkv[:, lanes_of(GROUPS * i + b)].astype(F32) * inverse
-            d = grad[:, lanes_of(b)]
-            high, low = split(unit * d)
-            along = nn(high, block_ref[...]) + nn(low, block_ref[...])
-            dqkv[:, lanes_of(GROUPS * i + b)] = (inverse * (d - unit * along)).astype(BF)
-
-    for t in y_peers:
-        arrived(far_qg.at[core, t], r_fqg.at[t])
-    send(far_qg.at[core], far_qg.at[core], r_cqg, partner)
+            dqkv[:, lanes_of(GROUPS * i + b)] = through(inverse, unit, grad[:, lanes_of(b)]).astype(BF)
+
+    hand_over(far_qg, r_fqg, r_cqg)
 
     for t in z_peers:
         arrived(far_sz.at[t], r_sz.at[t])
@@ -441,17 +449,6 @@
         dk[:, lanes_of(b)] += unnear(k_part, b)
         dv[:, lanes_of(b)] += unnear(v_part, b)
 
-    arrived(far_qg.at[other], r_cqg)
-    for t in y_peers:
-        arrived(far_s.at[core, t], r_fs.at[core, t])
-    for t in range(NY):
-        arrived(far_s.at[other, t], r_fs.at[other, t])
-    columns = far_s[...].reshape(TOK, 128).T
-    for b in range(GROUPS):
-        k_part, v_part = key_side(far_k, far_v, far_rows_of(far_qg, 0), far_rows_of(far_qg, 1), columns, b)
-        dk[:, lanes_of(b)] += unfar(k_part, b)
-        dv[:, lanes_of(b)] += unfar(v_part, b)
-
     unnormalize(inv_k, dk, 1)
     dqkv[:, 2 * WIDTH :] = dv[...].astype(BF)
     dqkv_t[WIDTH:, :] = dqkv[:, WIDTH:].T
@@ -463,6 +460,44 @@
     for o in owners:
         send(late_out.at[o], late_in.at[own], r_late.at[own], owner(o))
     late_in[own] = late_out[own]
+
+    far_inverse, far_unit = [], []
+    for b in range(GROUPS):
+        high, low = split(inv_k[:, lanes_of(b)])
+        mask = far_bf[:, lanes_of(b)]
+        inverse = nn(take_far, high * mask) + nn(take_far, low * mask)
+        far_inverse.append(inverse)
+        far_unit.append(nn(take_far, qkv[:, lanes_of(GROUPS + b)] * mask) * inverse)
+    n = iota((LATE, 1), 0)
+    t = sum((n >= QOWN * i).astype(jnp.int32) for i in range(1, NY - 1))
+    left = n - QOWN * t
+    u = sum((left >= QOWN // NZ * i).astype(jnp.int32) for i in range(1, NZ))
+    column = QROWS * (1 + t) + (QROWS // NZ) * u + (QOWN // NZ) * own + (left - QOWN // NZ * u) - WIDTH
+    column = jnp.where(n < QOWN * (NY - 1), column, -1)
+    chosen[...] = (iota((LATE, 2 * WIDTH), 1) == column).astype(F32).astype(BF)
+    offsets = jnp.concatenate([far_row, far_row], axis=1).astype(F32).astype(BF)
+    offsets = nt(chosen[...], jnp.broadcast_to(offsets, (16, 2 * WIDTH)))[:, :1]
+    far_place = ((iota((LATE, 128), 1) & (TOK // FAR - 1)).astype(F32) == offsets).astype(F32)
+    far_place = jnp.concatenate([far_place] * OWNERS, axis=1)
+    spread_rows = (iota((16, OWNERS * TOK), 1) // (TOK // FAR) == iota((16, OWNERS * TOK), 0)).astype(F32).astype(BF)
+
+    for t in range(NY):
+        arrived(far_qg.at[other, t], r_cqg.at[t])
+    for t in y_peers:
+        arrived(far_s.at[core, t], r_fs.at[core, t])
+    for t in range(NY):
+        arrived(far_s.at[other, t], r_fs.at[other, t])
+    columns = far_s[...].reshape(TOK, 128).T
+    k_far, v_far = [], []
+    for b in range(GROUPS):
+        k_part, v_part = key_side(far_k, far_v, far_rows_of(far_qg, 0), far_rows_of(far_qg, 1), columns, b)
+        k_far.append(through(far_inverse[b], far_unit[b], k_part))
+        v_far.append(v_part)
+    two_rows = [jnp.concatenate(parts, axis=1) for parts in (k_far, v_far)]
+    corr[own] = packed(two_rows)
+    for o in owners:
+        send(corr.at[own], corr.at[own], r_corr.at[own], owner(o))
+
     for o in owners:
         arrived(early_in.at[o], r_early.at[o])
     for t in range(NX):
@@ -475,10 +510,15 @@
     o_sum[...] = nn(factors(early_in, slice(0, NY * OOWN)), cots[...].reshape(OWNERS * TOK, WIDTH))
     tokens = toks[...].reshape(OWNERS * TOK, WIDTH)
     q_sum[: EARLY - NY * OOWN, :] = nn(factors(early_in, slice(NY * OOWN, EARLY)), tokens)
-    grad_tok_ref[...] = nn(dqkv[...], wqkv_ref[...]).astype(BF)
+
     for o in owners:
         arrived(late_in.at[o], r_late.at[o])
-    late = nn(factors(late_in, slice(0, LATE)), tokens)
+    for o in owners:
+        arrived(corr.at[o], r_corr.at[o])
+    ordered = nn(order_ref[...], corr[...].reshape(OWNERS * PACK, 128)).astype(BF)
+    ordered = jnp.concatenate([ordered[16 * t : 16 * (t + 1)] for t in range(2 * TILES)], axis=1)
+    added = nn(nt(chosen[...], ordered).astype(BF), spread_rows) * far_place
+    late = nn((factors(late_in, slice(0, LATE)).astype(F32) + added).astype(BF), tokens)
     q_sum[QOWN:, :] = late[: (NY - 1) * QOWN]
 
     y_right, y_left = at(lax.rem(y + 1, NY), z, core), at(lax.rem(y + NY - 1, NY), z, core)
@@ -503,6 +543,11 @@
     right_part, left_part = piece(lax.rem(y + 1, NY)), piece(lax.rem(y + NY - 1, NY))
     y_out(2, right_part[b_], y_right)
     y_out(4, left_part[a], y_left)
+    for i, rows in enumerate(two_rows):
+        for b in range(GROUPS):
+            at_lanes = lanes_of(GROUPS * (1 + i) + b)
+            dqkv[:, at_lanes] = (dqkv[:, at_lanes].astype(F32) + unfar(rows[:, lanes_of(b)], b)).astype(BF)
+    grad_tok_ref[...] = nn(dqkv[...], wqkv_ref[...]).astype(BF)
     y_out(3, right_part[a] + y_in(0), y_right)
     y_out(5, left_part[b_] + y_in(1), y_left)
     part = piece(y)
@@ -594,14 +639,15 @@
             held(NZ, PACK, 128), held(NZ, PACK, 128),
             held(2, NY, 2, 16, WIDTH), held(2, NY, 2, 16, WIDTH), held_f32(NZ, 16, 128), held_f32(2, NY, 16, 128),
             held(WIDTH, TOK), held(3 * WIDTH, TOK), held_f32(OWNERS, LATE, 128),
+            held(OWNERS, PACK, 128), held(LATE, 2 * WIDTH),
             held(OWNERS, EARLY, 128), held(OWNERS, EARLY, 128), held(OWNERS, LATE, 128), held(OWNERS, LATE, 128),
             held_f32(NY * QOWN, WIDTH), held_f32(NY * OOWN, WIDTH),
             held(6, PIECE // 2, WIDTH), held(6, PIECE // 2, WIDTH),
             held(NZ, 16, WIDTH), held(NZ, 16, WIDTH),
-            dma((24,)), dma((112,)),
+            dma((24,)), dma((128,)),
             dma((4,)), dma((4,)), dma((4,)), dma((4,)),
-            dma((8,)), dma((8,)), dma((8,)), dma((8,)), dma((8,)), dma((8,)), dma((4,)), dma((4,)), dma, dma,
-            dma((2, 4)), dma((8,)), dma((8,)), dma((6,)), dma((8,)),
+            dma((8,)), dma((8,)), dma((8,)), dma((8,)), dma((8,)), dma((8,)), dma((4,)), dma((4,)), dma((4,)), dma((4,)),
+            dma((2, 4)), dma((8,)), dma((8,)), dma((8,)), dma((6,)), dma((8,)),
         ],
         compiler_params=pltpu.CompilerParams(
             collective_id=0, has_side_effects=True, vmem_limit_bytes=56 * 1024 * 1024

time: 64.9 us -> 66.4 us (1.023)
  the two profiles are of different devices: /device:TPU:16 before, /device:TPU:1 now
where the time goes in v4:
time: 66.4 us; the launch traced here: 65 us
  Pallas kernels  61 us (92%)
  local copies, waits for them, and re-layouts  3.35 us (5%)
    pallas_call x1, Pallas kernels, body(): pl.pallas_call(layer, out_shape=results, in_specs=[smem] * 3 + [hbm] * 10...  60.2 us
    unnamed x8, local copies, waits for them, and re-layouts  3.35 us

profile of v4, /device:TPU:1, one launch (start us, length us, event | category | flops | bytes accessed | tf_op | source)
XLA Modules:
  0.0 65.0 jit_solution(4008231675782437937)
XLA Ops:
  0.6 60.2 %shard_map.156 = (bf16[128,768]{1,0:T(8,128)(2,1)}, bf16[128,768]{1,0:T(8,128)(2,1)}, f32[9,768]{1,0:T(8,128)}, f32[3,768]{1,0:T(4,128)}) custom-call(f32[12]{0:T(128)} %scale_ref.1, s32[12]{0:T(128)} %near_ref.1, s32[12]{0:T(128)} %far_ref.1, bf16[128,768]{1,0:T(8,128)(2,1)} %bitcast.4, bf16[128,768]{1,0:T(8,128)(2,1)} %bitcast.5, ...), custom_call_target="tpu_custom_call" | custom-call | tf_op jit(solution)/shard_map/pallas_call | solution.py:627
  60.9 0.0 copy-start
  60.9 0.9 %copy-done = bf16[128,768]{1,0:T(8,128)(2,1)S(1)} copy-done((bf16[128,768]{1,0:T(8,128)(2,1)S(1)}, bf16[128,768]{1,0:T(8,128)(2,1)}, u32[]{:S(2)}) %copy-start) | copy-done | bytes 196632
  61.8 0.0 copy-start.1
  61.8 0.9 %copy-done.1 = bf16[128,768]{1,0:T(8,128)(2,1)S(1)} copy-done((bf16[128,768]{1,0:T(8,128)(2,1)S(1)}, bf16[128,768]{1,0:T(8,128)(2,1)}, u32[]{:S(2)}) %copy-start.1) | copy-done | bytes 196632
  62.7 0.0 copy-start.2
  62.7 0.8 %copy-done.2 = f32[9,768]{1,0:T(8,128)S(1)} copy-done((f32[9,768]{1,0:T(8,128)S(1)}, f32[9,768]{1,0:T(8,128)}, u32[]{:S(2)}) %copy-start.2) | copy-done | bytes 27672
  63.5 0.0 copy-start.3
  63.5 0.7 %copy-done.3 = f32[3,768]{1,0:T(4,128)S(1)} copy-done((f32[3,768]{1,0:T(4,128)S(1)}, f32[3,768]{1,0:T(4,128)}, u32[]{:S(2)}) %copy-start.3) | copy-done | bytes 9240
  64.2 0.8 %shard_map.157 = (bf16[128,768]{1,0:T(8,128)(2,1)}, bf16[128,768]{1,0:T(8,128)(2,1)}, f32[9,768]{1,0:T(8,128)}, f32[3,768]{1,0:T(4,128)}) custom-call(bf16[128,768]{1,0:T(8,128)(2,1)S(1)} %copy-done, bf16[128,768]{1,0:T(8,128)(2,1)S(1)} %copy-done.1, f32[9,768]{1,0:T(8,128)S(1)} %copy-done.2, f32[3,768]{1,0:T(4,128)S(1)} %copy-done.3), custom_call_target="tpu_custom_call" | custom-call | tf_op jit(solution)/shard_map/pallas_call | solution.py:656
Async XLA Ops:
  60.9 0.9 %copy-start = (bf16[128,768]{1,0:T(8,128)(2,1)S(1)}, bf16[128,768]{1,0:T(8,128)(2,1)}, u32[]{:S(2)}) copy-start(bf16[128,768]{1,0:T(8,128)(2,1)} %get-tuple-element.12.refs_0_) | copy-start | bytes 589828
  61.8 0.9 %copy-start.1 = (bf16[128,768]{1,0:T(8,128)(2,1)S(1)}, bf16[128,768]{1,0:T(8,128)(2,1)}, u32[]{:S(2)}) copy-start(bf16[128,768]{1,0:T(8,128)(2,1)} %get-tuple-element.13.refs_1_) | copy-start | bytes 589828
  62.7 0.8 %copy-start.2 = (f32[9,768]{1,0:T(8,128)S(1)}, f32[9,768]{1,0:T(8,128)}, u32[]{:S(2)}) copy-start(f32[9,768]{1,0:T(8,128)} %get-tuple-element.14.refs_2_) | copy-start | bytes 82948
  63.5 0.7 %copy-start.3 = (f32[3,768]{1,0:T(4,128)S(1)}, f32[3,768]{1,0:T(4,128)}, u32[]{:S(2)}) copy-start(f32[3,768]{1,0:T(4,128)} %get-tuple-element.15.refs_3_) | copy-start | bytes 27652

commit v5 on v4

--- a/solution.py
+++ b/solution.py
@@ -25,6 +25,8 @@
 PACK = 32
 TILES = WIDTH // 128
 OWNERS = 2 * NX
+CUT = 512
+REST = WIDTH - CUT
 QROWS = 3 * WIDTH // NY
 OROWS = WIDTH // NY
 QOWN, OOWN = QROWS // OWNERS, OROWS // OWNERS
@@ -75,14 +77,15 @@
 
 def layer(
     scale_ref, near_ref, far_ref, tok_hbm, cot_hbm, wqkv_hbm, wout_hbm,
-    block_hbm, compact_hbm, order_hbm, perm_q_hbm, perm_o_hbm, deal_hbm,
+    block_hbm, compact_hbm, order_hbm, perm_q_hbm, perm_o_hbm, deal_hbm, deal_b_hbm, deal_y_hbm,
     branch_ref, grad_tok_ref, qkv_out, out_out,
-    wqkv_ref, wout_ref, block_ref, compact_ref, order_ref, perm_q, perm_o, deal_ref,
+    wqkv_ref, wout_ref, block_ref, compact_ref, order_ref, perm_q, perm_o, deal_ref, deal_b_ref, deal_y_ref,
     toks, cots, qkv, qn, kn, gr, inv_q, inv_k, p_loc, p_near, p_far, num, den, dq, dk, dv, dqkv, pack,
     near_kv, near_qg, near_s, far_zkv, far_zqg, far_kv, far_qg, far_sz, far_s,
-    attn_t, dqkv_t, stage, corr, chosen, early_out, early_in, late_out, late_in, q_sum, o_sum, y_send, y_recv, z_send, z_recv,
+    attn_t, dqkv_t, stage, corr, chosen, early_out, early_in, late_out, late_in, q_sum, o_sum, b_part,
+    a_y_send, a_y_recv, a_z_send, a_z_recv, b_z_send, b_z_recv, b_y_send, b_y_recv,
     loads, sends, r_tok, r_cot, r_ftok, r_fcot, r_nkv, r_nqg, r_ns, r_zkv, r_zqg, r_sz, r_fkv, r_fqg, r_ckv, r_cqg,
-    r_fs, r_early, r_late, r_corr, r_y, r_z,
+    r_fs, r_early, r_late, r_corr, r_ay, r_az, r_bz, r_by,
 ):
     seq, core, z, y = place()
     x = lax.axis_index("dp")
@@ -219,6 +222,9 @@
     leave((kn[...], qkv[:, 2 * WIDTH :]), far_zkv, near_kv)
     for t in z_peers:
         send(far_zkv.at[z], far_zkv.at[z], r_zkv.at[z], at(y, t, core))
+    for t in near_same:
+        send(near_kv.at[mine], near_kv.at[mine], r_nkv.at[mine], {"seq": base + t})
+    send(near_kv.at[mine], near_kv.at[mine], r_nkv.at[mine], partner)
 
     first = len(loading)
     load(order_hbm, order_ref)
@@ -226,6 +232,8 @@
     load(perm_q_hbm, perm_q)
     load(perm_o_hbm, perm_o)
     load(deal_hbm, deal_ref)
+    load(deal_b_hbm, deal_b_ref)
+    load(deal_y_hbm, deal_y_ref)
     for copy in loading[2 + 2 * GROUPS : first]:
         copy.wait()
     cot = cots[own]
@@ -236,9 +244,8 @@
         inv_q[:, lanes_of(b)] = inverse
         qn[:, lanes_of(b)] = unit.astype(BF)
     leave((qn[...], gr[...]), far_zqg, near_qg)
-    for t in near_same:
-        send(near_kv.at[mine], near_kv.at[mine], r_nkv.at[mine], {"seq": base + t})
-    send(near_kv.at[mine], near_kv.at[mine], r_nkv.at[mine], partner)
+    for t in z_peers:
+        send(far_zqg.at[z], far_zqg.at[z], r_zqg.at[z], at(y, t, core))
     for all_, recv, forward_recv in ((toks, r_tok, r_ftok), (cots, r_cot, r_fcot)):
         for t in x_peers:
             send(all_.at[own], all_.at[own], recv.at[x], {"seq": seq, "dp": t})
@@ -304,8 +311,6 @@
 
     along_y(far_zkv, r_zkv, far_kv, r_fkv)
     across(near_kv, r_nkv)
-    for t in z_peers:
-        send(far_zqg.at[z], far_zqg.at[z], r_zqg.at[z], at(y, t, core))
     for t in near_same:
         send(near_qg.at[mine], near_qg.at[mine], r_nqg.at[mine], {"seq": base + t})
     send(near_qg.at[mine], near_qg.at[mine], r_nqg.at[mine], partner)
@@ -316,7 +321,6 @@
         num[:, lanes_of(b)] += unnear(n_part, b)
         den[:, lanes_of(b)] += unnear(d_part, b)
     hand_over(far_kv, r_fkv, r_ckv)
-    along_y(far_zqg, r_zqg, far_qg, r_fqg)
     for t in range(NY):
         arrived(far_kv.at[other, t], r_ckv.at[t])
     far_k, far_v, far_q, far_g = far_rows
@@ -333,17 +337,21 @@
     high, low = split(slim)
 
     def take(selection, mask):
-        return nn(selection, high * mask) + nn(selection, low * mask)
-
-    far_sz[z] = take(take_far_z, far_slim)
+        first, second = nn(selection, high * mask), nn(selection, low * mask)
+        return first + second, (first + pltpu.roll(second, 64, 1)).astype(BF)
+
+    def joined(rows):
+        columns = rows.astype(F32).reshape(TOK, 128).T
+        return columns[:64] + columns[64:]
+
+    far_sz[z] = take(take_far_z, far_slim)[1]
     for t in z_peers:
         send(far_sz.at[z], far_sz.at[z], r_sz.at[z], at(y, t, core))
-    near_slim_rows = take(take_near, near_slim)
-    far_slim_rows = take(take_far, far_slim)
-    near_s[mine] = near_slim_rows
+    near_slim_rows, near_s[mine] = take(take_near, near_slim)
+    far_slim_rows = take(take_far, far_slim)[0]
     for t in near_peers:
         send(near_s.at[mine], near_s.at[mine], r_ns.at[mine], {"seq": base + t})
-    across(near_qg, r_nqg)
+    along_y(far_zqg, r_zqg, far_qg, r_fqg)
 
     for b in range(GROUPS):
         g = spread(gr[:, lanes_of(b)])
@@ -386,16 +394,6 @@
             unit = qkv[:, lanes_of(GROUPS * i + b)].astype(F32) * inverse
             dqkv[:, lanes_of(GROUPS * i + b)] = through(inverse, unit, grad[:, lanes_of(b)]).astype(BF)
 
-    hand_over(far_qg, r_fqg, r_cqg)
-
-    for t in z_peers:
-        arrived(far_sz.at[t], r_sz.at[t])
-    far_s[core, y] = jnp.sum(far_sz[...], axis=0)
-    for t in y_peers:
-        send(far_s.at[core, y], far_s.at[core, y], r_fs.at[core, y], at(t, z, core))
-        send(far_s.at[core, y], far_s.at[core, y], r_fs.at[core, y], at(t, z, other))
-    send(far_s.at[core, y], far_s.at[core, y], r_fs.at[core, y], partner)
-
     unnormalize(inv_q, dq, 0)
     attn_t[...] = attn.T
     dqkv_t[:WIDTH, :] = dqkv[:, :WIDTH].T
@@ -416,12 +414,6 @@
     for o in owners:
         send(early_out.at[o], early_in.at[own], r_early.at[own], owner(o))
     early_in[own] = early_out[own]
-    branch_ref[...] = nn(attn, wout_ref[...]).astype(BF)
-
-    for all_, recv, forward_recv in ((toks, r_tok, r_ftok), (cots, r_cot, r_fcot)):
-        for t in x_peers:
-            arrived(all_.at[core * NX + t], recv.at[t])
-            send(all_.at[core * NX + t], all_.at[core * NX + t], forward_recv.at[t], partner)
 
     def key_side(keys, values, queries, grads, columns, b):
         q, g = queries(b), grads(b)
@@ -438,16 +430,25 @@
         p, d = jnp.concatenate(ps, axis=0).astype(BF), jnp.concatenate(ds, axis=0).astype(BF)
         return fold(nn(d, q)), fold(nn(p, g))
 
+    across(near_qg, r_nqg)
     for t in near_peers:
         arrived(near_s.at[t], r_ns.at[t])
     for t in near_other:
         arrived(near_qg.at[t], r_nqg.at[t])
-    columns = near_s[...].reshape(TOK, 128).T
+    columns = joined(near_s[...])
     near_k, near_v = near_kv[mine, 0], near_kv[mine, 1]
     for b in range(GROUPS):
         k_part, v_part = key_side(near_k, near_v, near_rows(near_qg, 0), near_rows(near_qg, 1), columns, b)
         dk[:, lanes_of(b)] += unnear(k_part, b)
         dv[:, lanes_of(b)] += unnear(v_part, b)
+
+    for t in z_peers:
+        arrived(far_sz.at[t], r_sz.at[t])
+    far_s[core, y] = jnp.sum(far_sz[...].astype(F32), axis=0).astype(BF)
+    for t in y_peers:
+        send(far_s.at[core, y], far_s.at[core, y], r_fs.at[core, y], at(t, z, core))
+        send(far_s.at[core, y], far_s.at[core, y], r_fs.at[core, y], at(t, z, other))
+    send(far_s.at[core, y], far_s.at[core, y], r_fs.at[core, y], partner)
 
     unnormalize(inv_k, dk, 1)
     dqkv[:, 2 * WIDTH :] = dv[...].astype(BF)
@@ -460,6 +461,13 @@
     for o in owners:
         send(late_out.at[o], late_in.at[own], r_late.at[own], owner(o))
     late_in[own] = late_out[own]
+
+    hand_over(far_qg, r_fqg, r_cqg)
+    branch_ref[...] = nn(attn, wout_ref[...]).astype(BF)
+    for all_, recv, forward_recv in ((toks, r_tok, r_ftok), (cots, r_cot, r_fcot)):
+        for t in x_peers:
+            arrived(all_.at[core * NX + t], recv.at[t])
+            send(all_.at[core * NX + t], all_.at[core * NX + t], forward_recv.at[t], partner)
 
     far_inverse, far_unit = [], []
     for b in range(GROUPS):
@@ -487,7 +495,7 @@
         arrived(far_s.at[core, t], r_fs.at[core, t])
     for t in range(NY):
         arrived(far_s.at[other, t], r_fs.at[other, t])
-    columns = far_s[...].reshape(TOK, 128).T
+    columns = joined(far_s[...])
     k_far, v_far = [], []
     for b in range(GROUPS):
         k_part, v_part = key_side(far_k, far_v, far_rows_of(far_qg, 0), far_rows_of(far_qg, 1), columns, b)
@@ -521,59 +529,67 @@
     late = nn((factors(late_in, slice(0, LATE)).astype(F32) + added).astype(BF), tokens)
     q_sum[QOWN:, :] = late[: (NY - 1) * QOWN]
 
-    y_right, y_left = at(lax.rem(y + 1, NY), z, core), at(lax.rem(y + NY - 1, NY), z, core)
-    a, b_ = slice(0, PIECE // 2), slice(PIECE // 2, PIECE)
-
-    def piece(t):
-        q_rows = pl.ds(pl.multiple_of(t * QOWN, 8), QOWN)
-        o_rows = pl.ds(pl.multiple_of(t * OOWN, 8), OOWN)
-        return jnp.concatenate([q_sum[q_rows, :], o_sum[o_rows, :]], axis=0)
-
-    def y_out(slot, part, device):
-        y_send[slot] = part.astype(BF)
-        send(y_send.at[slot], y_recv.at[slot], r_y.at[slot], device)
-
-    def y_in(slot):
-        arrived(y_recv.at[slot], r_y.at[slot])
-        return y_recv[slot].astype(F32)
-
-    part = piece(lax.rem(y + 2, NY))
-    y_out(0, part[a], y_right)
-    y_out(1, part[b_], y_left)
-    right_part, left_part = piece(lax.rem(y + 1, NY)), piece(lax.rem(y + NY - 1, NY))
-    y_out(2, right_part[b_], y_right)
-    y_out(4, left_part[a], y_left)
+    left, right = slice(0, CUT), slice(CUT, WIDTH)
+    for t in range(NY):
+        yz_part = jnp.concatenate(
+            [q_sum[t * QOWN : (t + 1) * QOWN, :], o_sum[t * OOWN : (t + 1) * OOWN, :]], axis=0
+        ).astype(BF)
+        a_y_send[t] = yz_part[:, left]
+        b_part[t * PIECE : (t + 1) * PIECE, :] = yz_part[:, right]
+    for t in y_peers:
+        send(a_y_send.at[t], a_y_recv.at[y], r_ay.at[y], at(t, z, core))
+    a_y_recv[y] = a_y_send[y]
+    dealt = nn(deal_b_ref[...], b_part[...]).astype(BF)
+    for t in range(NZ):
+        b_z_send[t] = dealt[48 * t : 48 * (t + 1), :]
+    for t in z_peers:
+        send(b_z_send.at[t], b_z_recv.at[z], r_bz.at[z], at(y, t, core))
+    b_z_recv[z] = b_z_send[z]
+
     for i, rows in enumerate(two_rows):
         for b in range(GROUPS):
             at_lanes = lanes_of(GROUPS * (1 + i) + b)
             dqkv[:, at_lanes] = (dqkv[:, at_lanes].astype(F32) + unfar(rows[:, lanes_of(b)], b)).astype(BF)
     grad_tok_ref[...] = nn(dqkv[...], wqkv_ref[...]).astype(BF)
-    y_out(3, right_part[a] + y_in(0), y_right)
-    y_out(5, left_part[b_] + y_in(1), y_left)
-    part = piece(y)
-    part = jnp.concatenate([part[a] + y_in(4) + y_in(3), part[b_] + y_in(2) + y_in(5)], axis=0)
-
+
+    for t in y_peers:
+        arrived(a_y_recv.at[t], r_ay.at[t])
+    part = jnp.sum(a_y_recv[...].astype(F32), axis=0)
     dealt = nn(deal_ref[...], part.astype(BF)).astype(BF)
     for t in range(NZ):
-        z_send[t] = dealt[16 * t : 16 * (t + 1), :]
+        a_z_send[t] = dealt[16 * t : 16 * (t + 1), :]
     for t in z_peers:
-        send(z_send.at[t], z_recv.at[z], r_z.at[z], at(y, t, core))
-    z_recv[z] = z_send[z]
+        send(a_z_send.at[t], a_z_recv.at[z], r_az.at[z], at(y, t, core))
+    a_z_recv[z] = a_z_send[z]
     for t in z_peers:
-        arrived(z_recv.at[t], r_z.at[t])
-    share = jnp.sum(z_recv[...].astype(F32), axis=0)
-    qkv_out[...] = share[: QOWN // NZ]
-    out_out[...] = share[QOWN // NZ : PIECE // NZ]
+        arrived(b_z_recv.at[t], r_bz.at[t])
+    part = jnp.sum(b_z_recv[...].astype(F32), axis=0)
+    dealt = nn(deal_y_ref[...], part.astype(BF)).astype(BF)
+    for t in range(NY):
+        b_y_send[t] = dealt[16 * t : 16 * (t + 1), :]
+    for t in y_peers:
+        send(b_y_send.at[t], b_y_recv.at[y], r_by.at[y], at(t, z, core))
+    b_y_recv[y] = b_y_send[y]
+    for columns, ref, recv, peers in ((left, a_z_recv, r_az, z_peers), (right, b_y_recv, r_by, y_peers)):
+        for t in peers:
+            arrived(ref.at[t], recv.at[t])
+        share = jnp.sum(ref[...].astype(F32), axis=0)
+        qkv_out[:, columns] = share[: QOWN // NZ]
+        out_out[:, columns] = share[QOWN // NZ : PIECE // NZ]
     for copy in sent:
         copy.wait_send()
 
 
 def finish(*refs):
-    count = len(refs) // 2
-    copies = [pltpu.make_async_copy(refs[n], refs[count + n], refs[-1].at[n]) for n in range(count)]
-    for copy in copies:
+    sources, results, held, sems = refs[:4], refs[4:8], refs[8:12], refs[12]
+    inward = [pltpu.make_async_copy(sources[n], held[n], sems.at[0, n]) for n in range(4)]
+    outward = [pltpu.make_async_copy(held[n], results[n], sems.at[1, n]) for n in range(4)]
+    for copy in inward:
         copy.start()
-    for copy in copies:
+    for come, go in zip(inward, outward):
+        come.wait()
+        go.start()
+    for copy in outward:
         copy.wait()
 
 
@@ -600,7 +616,14 @@
             deal[t * 16 + i, t * 9 + i] = 1
         for i in range(3):
             deal[t * 16 + 9 + i, QOWN + t * 3 + i] = 1
-    return [jnp.asarray(m, BF) for m in (block, compact, order, deal_out(9), deal_out(3), deal)]
+    deal_b = np.zeros((NZ * 48, NY * PIECE), np.float32)
+    deal_y = np.zeros((NY * 16, 48), np.float32)
+    for s in range(NY):
+        for i in range(12):
+            deal_y[s * 16 + i, s * 12 + i] = 1
+            for t in range(NZ):
+                deal_b[t * 48 + s * 12 + i, s * PIECE + (t * 9 + i if i < 9 else QOWN + t * 3 + i - 9)] = 1
+    return [jnp.asarray(m, BF) for m in (block, compact, order, deal_out(9), deal_out(3), deal, deal_b, deal_y)]
 
 
 def body(tokens, cotangent, qkv_weight, out_weight, logit_scale, near_offsets, far_offsets):
@@ -627,7 +650,7 @@
     values = pl.pallas_call(
         layer,
         out_shape=results,
-        in_specs=[smem] * 3 + [hbm] * 10,
+        in_specs=[smem] * 3 + [hbm] * (4 + len(fixed)),
         out_specs=[vmem] * 4,
         scratch_shapes=[
             held(3 * WIDTH, WIDTH), held(WIDTH, WIDTH), *[held(*m.shape) for m in fixed],
@@ -635,19 +658,20 @@
             held(TOK, 3 * WIDTH), wide_bf, wide_bf, wide_bf, wide, wide,
             held_f32(HEADS * TOK, 128), held_f32(GROUPS, GROUP * 16, 128), held_f32(GROUPS, GROUP * 16, 128),
             wide, wide, wide, wide, wide, held(TOK, 3 * WIDTH), held_f32(PACK, 128),
-            held(SPAN, 2, NEAR, WIDTH), held(SPAN, 2, NEAR, WIDTH), held_f32(SPAN, NEAR, 128),
+            held(SPAN, 2, NEAR, WIDTH), held(SPAN, 2, NEAR, WIDTH), held(SPAN, NEAR, 128),
             held(NZ, PACK, 128), held(NZ, PACK, 128),
-            held(2, NY, 2, 16, WIDTH), held(2, NY, 2, 16, WIDTH), held_f32(NZ, 16, 128), held_f32(2, NY, 16, 128),
+            held(2, NY, 2, 16, WIDTH), held(2, NY, 2, 16, WIDTH), held(NZ, 16, 128), held(2, NY, 16, 128),
             held(WIDTH, TOK), held(3 * WIDTH, TOK), held_f32(OWNERS, LATE, 128),
             held(OWNERS, PACK, 128), held(LATE, 2 * WIDTH),
             held(OWNERS, EARLY, 128), held(OWNERS, EARLY, 128), held(OWNERS, LATE, 128), held(OWNERS, LATE, 128),
             held_f32(NY * QOWN, WIDTH), held_f32(NY * OOWN, WIDTH),
-            held(6, PIECE // 2, WIDTH), held(6, PIECE // 2, WIDTH),
-            held(NZ, 16, WIDTH), held(NZ, 16, WIDTH),
+            held(NY * PIECE, REST),
+            held(NY, PIECE, CUT), held(NY, PIECE, CUT), held(NZ, 16, CUT), held(NZ, 16, CUT),
+            held(NZ, 48, REST), held(NZ, 48, REST), held(NY, 16, REST), held(NY, 16, REST),
             dma((24,)), dma((128,)),
             dma((4,)), dma((4,)), dma((4,)), dma((4,)),
             dma((8,)), dma((8,)), dma((8,)), dma((8,)), dma((8,)), dma((8,)), dma((4,)), dma((4,)), dma((4,)), dma((4,)),
-            dma((2, 4)), dma((8,)), dma((8,)), dma((8,)), dma((6,)), dma((8,)),
+            dma((2, 4)), dma((8,)), dma((8,)), dma((8,)), dma((4,)), dma((8,)), dma((8,)), dma((4,)),
         ],
         compiler_params=pltpu.CompilerParams(
             collective_id=0, has_side_effects=True, vmem_limit_bytes=56 * 1024 * 1024
@@ -658,8 +682,8 @@
         out_shape=results,
         in_specs=[pl.BlockSpec(memory_space=pl.ANY)] * 4,
         out_specs=[pl.BlockSpec(memory_space=pl.ANY)] * 4,
-        scratch_shapes=[dma((4,))],
-        compiler_params=pltpu.CompilerParams(vmem_limit_bytes=1024 * 1024),
+        scratch_shapes=[pltpu.VMEM(r.shape, r.dtype) for r in results] + [dma((2, 4))],
+        compiler_params=pltpu.CompilerParams(vmem_limit_bytes=56 * 1024 * 1024),
     )(*values)
     return (branch[None], grad_inputs[None], qkv_share, out_share)
 

time: 66.4 us -> 60.6 us (0.913); the launches traced: 65 us -> 60.5 us
  local copies, waits for them, and re-layouts: 3.35 us -> 0 us
  Pallas kernels: 61 us -> 59.8 us
    unnamed x8 -> x0, local copies, waits for them, and re-layouts: 3.35 us -> none
    pallas_call x1, Pallas kernels: 60.2 us -> 58 us  [body(): pl.pallas_call(layer, out_shape=results, in_specs=[smem] * 3 + [hbm] * (4...]
    pallas_call x1, Pallas kernels: 0.78 us -> 1.78 us  [body(): pl.pallas_call(finish, out_shape=results, in_specs=[pl.BlockSpec(memory_s...]
where the time goes in v5:
time: 60.6 us; the launch traced here: 60.5 us
  Pallas kernels  59.8 us (99%)
  between operations  0.64 us (1%)
    pallas_call x1, Pallas kernels, body(): pl.pallas_call(layer, out_shape=results, in_specs=[smem] * 3 + [hbm] * (4...  58 us
    pallas_call x1, Pallas kernels, body(): pl.pallas_call(finish, out_shape=results, in_specs=[pl.BlockSpec(memory_s...  1.78 us

profile of v5, /device:TPU:1, one launch (start us, length us, event | category | flops | bytes accessed | tf_op | source)
XLA Modules:
  0.0 60.5 jit_solution(8478141552805276150)
XLA Ops:
  0.6 58.0 %shard_map.174 = (bf16[128,768]{1,0:T(8,128)(2,1)}, bf16[128,768]{1,0:T(8,128)(2,1)}, f32[9,768]{1,0:T(8,128)}, f32[3,768]{1,0:T(4,128)}) custom-call(f32[12]{0:T(128)} %scale_ref.1, s32[12]{0:T(128)} %near_ref.1, s32[12]{0:T(128)} %far_ref.1, bf16[128,768]{1,0:T(8,128)(2,1)} %bitcast.4, bf16[128,768]{1,0:T(8,128)(2,1)} %bitcast.5, ...), custom_call_target="tpu_custom_call" | custom-call | tf_op jit(solution)/shard_map/pallas_call | solution.py:650
  58.7 1.8 %shard_map.175 = (bf16[128,768]{1,0:T(8,128)(2,1)}, bf16[128,768]{1,0:T(8,128)(2,1)}, f32[9,768]{1,0:T(8,128)}, f32[3,768]{1,0:T(4,128)}) custom-call(bf16[128,768]{1,0:T(8,128)(2,1)} %get-tuple-element.12.refs_0_, bf16[128,768]{1,0:T(8,128)(2,1)} %get-tuple-element.13.refs_1_, f32[9,768]{1,0:T(8,128)} %get-tuple-element.14.refs_2_, ...), custom_call_target="tpu_custom_call" | custom-call | tf_op jit(solution)/shard_map/pallas_call | solution.py:680

commit v6 on v5

--- a/solution.py
+++ b/solution.py
@@ -76,10 +76,10 @@
 
 
 def layer(
-    scale_ref, near_ref, far_ref, tok_hbm, cot_hbm, wqkv_hbm, wout_hbm,
+    scale_hbm, near_hbm, far_hbm, tok_hbm, cot_hbm, wqkv_hbm, wout_hbm,
     block_hbm, compact_hbm, order_hbm, perm_q_hbm, perm_o_hbm, deal_hbm, deal_b_hbm, deal_y_hbm,
     branch_ref, grad_tok_ref, qkv_out, out_out,
-    wqkv_ref, wout_ref, block_ref, compact_ref, order_ref, perm_q, perm_o, deal_ref, deal_b_ref, deal_y_ref,
+    scale_ref, near_ref, far_ref, wqkv_ref, wout_ref, block_ref, compact_ref, order_ref, perm_q, perm_o, deal_ref, deal_b_ref, deal_y_ref,
     toks, cots, qkv, qn, kn, gr, inv_q, inv_k, p_loc, p_near, p_far, num, den, dq, dk, dv, dqkv, pack,
     near_kv, near_qg, near_s, far_zkv, far_zqg, far_kv, far_qg, far_sz, far_s,
     attn_t, dqkv_t, stage, corr, chosen, early_out, early_in, late_out, late_in, q_sum, o_sum, b_part,
@@ -101,22 +101,21 @@
         copy.start()
         loading.append(copy)
 
-    def load_rows(src, dst, start, stop):
-        for first in range(start, stop, LANES):
-            load(src.at[first : first + LANES], dst.at[first : first + LANES])
-
+    load(near_hbm, near_ref)
+    load(far_hbm, far_ref)
+    load(scale_hbm, scale_ref)
     load(tok_hbm, toks.at[own])
     load(block_hbm, block_ref)
-    load_rows(wqkv_hbm, wqkv_ref, WIDTH, 3 * WIDTH)
+    load(wqkv_hbm.at[WIDTH : 3 * WIDTH], wqkv_ref.at[WIDTH : 3 * WIDTH])
     load(cot_hbm, cots.at[own])
-    load_rows(wqkv_hbm, wqkv_ref, 0, WIDTH)
-    load_rows(wout_hbm, wout_ref, 0, WIDTH)
-
-    z_peers = [lax.rem(z + d, NZ) for d in range(1, NZ)]
-    y_peers = [lax.rem(y + d, NY) for d in range(1, NY)]
-    x_peers = [lax.rem(x + d, NX) for d in range(1, NX)]
+    load(wqkv_hbm.at[:WIDTH], wqkv_ref.at[:WIDTH])
+    load(wout_hbm, wout_ref)
+
+    z_peers = [lax.rem(z + d, NZ) for d in (4, 3, 5, 2, 6, 1, 7)]
+    y_peers = [lax.rem(y + d, NY) for d in (2, 1, 3)]
+    x_peers = [lax.rem(x + d, NX) for d in (2, 1, 3)]
     near_peers = [lax.rem(mine + d, SPAN) for d in range(1, SPAN)]
-    near_same = [2 * lax.rem(mine // 2 + d, SPAN // 2) + core for d in range(1, SPAN // 2)]
+    near_same = [2 * lax.rem(mine // 2 + d, SPAN // 2) + core for d in (2, 1, 3)]
     near_other = [2 * lax.rem(mine // 2 + d, SPAN // 2) + other for d in range(SPAN // 2)]
     partner = at(y, z, other)
     pair = seq - core
@@ -124,7 +123,7 @@
     def owner(o):
         return {"seq": pair + o // NX, "dp": lax.rem(o, NX)}
 
-    owners = [lax.rem(own + d, OWNERS) for d in range(1, OWNERS)]
+    owners = [lax.rem(own + d, OWNERS) for d in (2, 6, 1, 3, 5, 7, 4)]
     barrier = pltpu.get_barrier_semaphore()
     greeted = (
         [at(y, t, core) for t in z_peers]
@@ -157,6 +156,8 @@
         rows = x.shape[0] // GROUP
         return sum(x[h * rows : (h + 1) * rows] * picks_f[h] for h in range(GROUP))
 
+    for copy in loading[:3]:
+        copy.wait()
     wide_head = iota((1, WIDTH), 1) // HEAD
     slim_head = iota((1, 128), 1)
     slim_head = jnp.where(slim_head >= HEADS, slim_head - HEADS, slim_head)
@@ -208,11 +209,10 @@
         for i, x_ in enumerate(pair_of):
             near_into[mine, i] = nn(take_near, x_ * near_bf).astype(BF)
 
-    for copy in loading[:2]:
+    for copy in loading[3:6]:
         copy.wait()
     tok = toks[own]
     for b in range(GROUPS, 3 * GROUPS):
-        loading[2 + b - GROUPS].wait()
         qkv[:, lanes_of(b)] = nt(tok, wqkv_ref[lanes_of(b), :]).astype(BF)
     for b in range(GROUPS):
         inverse, unit = norms(qkv[:, lanes_of(GROUPS + b)])
@@ -234,7 +234,7 @@
     load(deal_hbm, deal_ref)
     load(deal_b_hbm, deal_b_ref)
     load(deal_y_hbm, deal_y_ref)
-    for copy in loading[2 + 2 * GROUPS : first]:
+    for copy in loading[6:first]:
         copy.wait()
     cot = cots[own]
     for b in range(GROUPS):
@@ -628,7 +628,6 @@
 
 def body(tokens, cotangent, qkv_weight, out_weight, logit_scale, near_offsets, far_offsets):
     fixed = constants()
-    smem = pl.BlockSpec(memory_space=pltpu.SMEM)
     hbm = pl.BlockSpec(memory_space=pltpu.HBM)
     vmem = pl.BlockSpec(memory_space=pltpu.VMEM)
     dma = pltpu.SemaphoreType.DMA
@@ -650,9 +649,10 @@
     values = pl.pallas_call(
         layer,
         out_shape=results,
-        in_specs=[smem] * 3 + [hbm] * (4 + len(fixed)),
+        in_specs=[hbm] * (7 + len(fixed)),
         out_specs=[vmem] * 4,
         scratch_shapes=[
+            pltpu.SMEM((HEADS,), F32), pltpu.SMEM((HEADS,), jnp.int32), pltpu.SMEM((HEADS,), jnp.int32),
             held(3 * WIDTH, WIDTH), held(WIDTH, WIDTH), *[held(*m.shape) for m in fixed],
             held(OWNERS, TOK, WIDTH), held(OWNERS, TOK, WIDTH),
             held(TOK, 3 * WIDTH), wide_bf, wide_bf, wide_bf, wide, wide,

time: 60.6 us -> 59.2 us (0.977)
  Pallas kernels: 59.8 us -> 58.5 us
    pallas_call x1, Pallas kernels: 58 us -> 56.7 us  [body(): pl.pallas_call(layer, out_shape=results, in_specs=[hbm] * (7 + len(fixed)...]
where the time goes in v6:
time: 59.2 us; the launch traced here: 59.1 us
  Pallas kernels  58.5 us (99%)
  between operations  0.64 us (1%)
    pallas_call x1, Pallas kernels, body(): pl.pallas_call(layer, out_shape=results, in_specs=[hbm] * (7 + len(fixed)...  56.7 us
    pallas_call x1, Pallas kernels, body(): pl.pallas_call(finish, out_shape=results, in_specs=[pl.BlockSpec(memory_s...  1.78 us

profile of v6, /device:TPU:1, one launch (start us, length us, event | category | flops | bytes accessed | tf_op | source)
XLA Modules:
  0.0 59.1 jit_solution(3811378374788150767)
XLA Ops:
  0.6 56.7 %shard_map.174 = (bf16[128,768]{1,0:T(8,128)(2,1)}, bf16[128,768]{1,0:T(8,128)(2,1)}, f32[9,768]{1,0:T(8,128)}, f32[3,768]{1,0:T(4,128)}) custom-call(f32[12]{0:T(128)} %scale_hbm.1, s32[12]{0:T(128)} %near_hbm.1, s32[12]{0:T(128)} %far_hbm.1, bf16[128,768]{1,0:T(8,128)(2,1)} %bitcast.4, bf16[128,768]{1,0:T(8,128)(2,1)} %bitcast.5, ...), custom_call_target="tpu_custom_call" | custom-call | tf_op jit(solution)/shard_map/pallas_call | solution.py:649
  57.3 1.8 %shard_map.175 = (bf16[128,768]{1,0:T(8,128)(2,1)}, bf16[128,768]{1,0:T(8,128)(2,1)}, f32[9,768]{1,0:T(8,128)}, f32[3,768]{1,0:T(4,128)}) custom-call(bf16[128,768]{1,0:T(8,128)(2,1)} %get-tuple-element.12.refs_0_, bf16[128,768]{1,0:T(8,128)(2,1)} %get-tuple-element.13.refs_1_, f32[9,768]{1,0:T(8,128)} %get-tuple-element.14.refs_2_, ...), custom_call_target="tpu_custom_call" | custom-call | tf_op jit(solution)/shard_map/pallas_call | solution.py:680

commit v7 on v6

--- a/solution.py
+++ b/solution.py
@@ -226,6 +226,13 @@
         send(near_kv.at[mine], near_kv.at[mine], r_nkv.at[mine], {"seq": base + t})
     send(near_kv.at[mine], near_kv.at[mine], r_nkv.at[mine], partner)
 
+    def over_x(ref, recv, forward_recv):
+        for t in x_peers:
+            send(ref.at[own], ref.at[own], recv.at[x], {"seq": seq, "dp": t})
+        send(ref.at[own], ref.at[own], forward_recv.at[x], partner)
+
+    over_x(toks, r_tok, r_ftok)
+
     first = len(loading)
     load(order_hbm, order_ref)
     load(compact_hbm, compact_ref)
@@ -244,12 +251,7 @@
         inv_q[:, lanes_of(b)] = inverse
         qn[:, lanes_of(b)] = unit.astype(BF)
     leave((qn[...], gr[...]), far_zqg, near_qg)
-    for t in z_peers:
-        send(far_zqg.at[z], far_zqg.at[z], r_zqg.at[z], at(y, t, core))
-    for all_, recv, forward_recv in ((toks, r_tok, r_ftok), (cots, r_cot, r_fcot)):
-        for t in x_peers:
-            send(all_.at[own], all_.at[own], recv.at[x], {"seq": seq, "dp": t})
-        send(all_.at[own], all_.at[own], forward_recv.at[x], partner)
+    over_x(cots, r_cot, r_fcot)
 
     ones = spread(jnp.ones((TOK, LANES), BF))
     for b in range(GROUPS):
@@ -311,6 +313,8 @@
 
     along_y(far_zkv, r_zkv, far_kv, r_fkv)
     across(near_kv, r_nkv)
+    for t in z_peers:
+        send(far_zqg.at[z], far_zqg.at[z], r_zqg.at[z], at(y, t, core))
     for t in near_same:
         send(near_qg.at[mine], near_qg.at[mine], r_nqg.at[mine], {"seq": base + t})
     send(near_qg.at[mine], near_qg.at[mine], r_nqg.at[mine], partner)

time: 59.2 us -> 57.8 us (0.976)
  Pallas kernels: 58.5 us -> 57 us
    pallas_call x1, Pallas kernels: 56.7 us -> 55.2 us  [body(): pl.pallas_call(layer, out_shape=results, in_specs=[hbm] * (7 + len(fixed)...]
where the time goes in v7:
time: 57.8 us; the launch traced here: 57.7 us
  Pallas kernels  57 us (99%)
  between operations  0.64 us (1%)
    pallas_call x1, Pallas kernels, body(): pl.pallas_call(layer, out_shape=results, in_specs=[hbm] * (7 + len(fixed)...  55.2 us
    pallas_call x1, Pallas kernels, body(): pl.pallas_call(finish, out_shape=results, in_specs=[pl.BlockSpec(memory_s...  1.78 us

profile of v7, /device:TPU:1, one launch (start us, length us, event | category | flops | bytes accessed | tf_op | source)
XLA Modules:
  0.0 57.7 jit_solution(13954038935163586216)
XLA Ops:
  0.6 55.2 %shard_map.174 = (bf16[128,768]{1,0:T(8,128)(2,1)}, bf16[128,768]{1,0:T(8,128)(2,1)}, f32[9,768]{1,0:T(8,128)}, f32[3,768]{1,0:T(4,128)}) custom-call(f32[12]{0:T(128)} %scale_hbm.1, s32[12]{0:T(128)} %near_hbm.1, s32[12]{0:T(128)} %far_hbm.1, bf16[128,768]{1,0:T(8,128)(2,1)} %bitcast.4, bf16[128,768]{1,0:T(8,128)(2,1)} %bitcast.5, ...), custom_call_target="tpu_custom_call" | custom-call | tf_op jit(solution)/shard_map/pallas_call | solution.py:653
  55.9 1.8 %shard_map.175 = (bf16[128,768]{1,0:T(8,128)(2,1)}, bf16[128,768]{1,0:T(8,128)(2,1)}, f32[9,768]{1,0:T(8,128)}, f32[3,768]{1,0:T(4,128)}) custom-call(bf16[128,768]{1,0:T(8,128)(2,1)} %get-tuple-element.12.refs_0_, bf16[128,768]{1,0:T(8,128)(2,1)} %get-tuple-element.13.refs_1_, f32[9,768]{1,0:T(8,128)} %get-tuple-element.14.refs_2_, ...), custom_call_target="tpu_custom_call" | custom-call | tf_op jit(solution)/shard_map/pallas_call | solution.py:684
